TPU v7x, 32 devices: a whole 2x2x4 slice. The times are simulated.
32 devices in a mesh: dp: 8 (over z, core), space: 4 (over y, x).
Axes of the slice: x: 2, y: 2, z: 4, core: 2. Of those that a mesh axis runs over, the one named last changes fastest.
Arguments:
- decoder_input: bfloat16 [8, 64, 8, 16, 128], P('dp', None, 'space'), may hold values from -6 to 6
- cotangent: bfloat16 [8, 64, 8, 16, 128], P('dp', None, 'space'), may hold values from -6 to 6
- encoder_input: bfloat16 [8, 64, 8, 16, 128], P('dp', None, 'space'), may hold values from -6 to 6
- decoder_weights: bfloat16 [2, 27, 4096], replicated, may hold values from -0.15625 to 0.15625
- other_grads: bfloat16 [8, 4, 12, 27, 4096], P('dp', 'space'), may hold values from -384 to 384
- assignment: int32 [12], replicated, may hold values from 0 to 15, as said below
- moment_first: float32 [16, 27, 4096], P('dp', None, 'space'), may hold values from -4 to 4
- moment_second: float32 [16, 27, 4096], P('dp', None, 'space'), may hold values from 0.02 to 2
- master_weights: float32 [16, 27, 4096], P('dp', None, 'space'), may hold values from -0.15625 to 0.15625
Outputs:
- input_grad: bfloat16 [8, 64, 8, 16, 128], P('dp', None, 'space')
- encoder_out: bfloat16 [8, 64, 8, 16, 128], P('dp', None, 'space')
- new_params: bfloat16 [12, 27, 4096], replicated
- new_first: float32 [16, 27, 4096], P('dp', None, 'space')
- new_second: float32 [16, 27, 4096], P('dp', None, 'space')
- new_master: float32 [16, 27, 4096], P('dp', None, 'space')
Inputs may be any that keep to these rules, and one draw needn't show every extreme that they name: `assignment`: the values are distinct; value j places the tensor with owner j // 2 in that owner's slot j % 2; some owner holds 2 tensors.
All inputs are finite; a program needn't handle non-finite values.
Results may differ from a plain program's by a relative error of at most 0.005.
Values may be sent and summed in bfloat16 or wider, within the bound.
A program may use at most 128 MiB of HBM per device.

v0:
```python
import math

import jax
import jax.numpy as jnp
from jax import lax
from jax.sharding import PartitionSpec as P

learn_rate = 0.002
decay_rate = 0.1
epsilon = 1e-08
bias_one = 1.0 - (0.9**50) ** 2
bias_two = 1.0 - (0.999**50) ** 2
volume_dims = ("NCDHW", "OIDHW", "NCDHW")
swapped_dims = ("CNDHW", "OIDHW", "NCDHW")


def padded_2(block, sides, width):
    for axis, dim in sides:
        count = lax.axis_size(axis)
        forward = [(i, i + 1) for i in range(count - 1)]
        forward.append((count - 1, 0))
        backward = [(target, source) for source, target in forward]
        low = lax.ppermute(
            lax.slice_in_dim(block, block.shape[dim] - width, None, axis=dim), axis, forward
        )
        high = lax.ppermute(lax.slice_in_dim(block, 0, width, axis=dim), axis, backward)
        block = jnp.concatenate([low, block, high], axis=dim)
    return block


def widened(field):
    rimmed = padded_2(field, (("space", 1),), 1)
    return jnp.pad(rimmed, ((0, 0), (0, 0), (1, 1), (1, 1)), mode="wrap")


def forward_local(padded, kernel):
    channels = kernel.shape[1]
    weights = kernel.reshape(3, 3, 3, channels, channels).transpose(3, 4, 0, 1, 2)
    result = lax.conv_general_dilated(
        padded[None],
        weights,
        (1, 1, 1),
        "VALID",
        dimension_numbers=volume_dims,
        preferred_element_type=jnp.float32,
    )
    return result[0].reshape(channels, -1)


def backward_local(padded, kernel):
    channels = kernel.shape[1]
    weights = kernel.reshape(3, 3, 3, channels, channels)[::-1, ::-1, ::-1].transpose(4, 3, 0, 1, 2)
    result = lax.conv_general_dilated(
        padded[None],
        weights,
        (1, 1, 1),
        "VALID",
        dimension_numbers=volume_dims,
        preferred_element_type=jnp.float32,
    )
    return result[0].reshape(channels, -1)


def kernel_grad(grad_field, padded):
    channels = grad_field.shape[0]
    result = lax.conv_general_dilated(
        padded[None],
        grad_field[:, None],
        (1, 1, 1),
        "VALID",
        dimension_numbers=swapped_dims,
        preferred_element_type=jnp.float32,
    )
    return result.transpose(2, 3, 4, 1, 0).reshape(27, channels, channels)


def per_device(
    decoder_input,
    cotangent,
    encoder_input,
    decoder_weights,
    other_grads,
    assignment,
    moment_first,
    moment_second,
    master_weights,
):
    field_shape = decoder_input.shape[1:]
    channels = field_shape[0]
    thick = field_shape[1]
    kernel_a = decoder_weights[0].reshape(27, channels, channels)
    kernel_b = decoder_weights[1].reshape(27, channels, channels)
    dec_field = decoder_input[0]
    dec_wide = widened(dec_field)
    preact = forward_local(dec_wide, kernel_a)
    sigma = jax.nn.sigmoid(preact)
    hidden = (preact * sigma).astype(jnp.bfloat16).reshape(field_shape)
    cot_field = cotangent[0]
    grad_b = kernel_grad(cot_field, widened(hidden))
    grad_hidden = backward_local(widened(cot_field), kernel_b)
    grad_pre = (
        (grad_hidden * sigma * (1.0 + preact * (1.0 - sigma)))
        .astype(jnp.bfloat16)
        .reshape(field_shape)
    )
    grad_a = kernel_grad(grad_pre, dec_wide)
    input_grad = backward_local(widened(grad_pre), kernel_a)
    input_grad = input_grad.astype(jnp.bfloat16).reshape((1,) + field_shape)
    replicas = lax.axis_size("dp")
    slabs = lax.axis_size("space")
    scale = 1.0 / math.sqrt(replicas * thick * slabs * field_shape[2] * field_shape[3])
    local_grads = other_grads[0, 0].astype(jnp.float32)
    local_grads = local_grads.at[0].add(grad_a.reshape(27, -1))
    local_grads = local_grads.at[1].add(grad_b.reshape(27, -1))
    local_grads = local_grads * scale
    slot_count = moment_first.shape[0]
    every_slot = replicas * slot_count
    padded_grads = (
        jnp.zeros((every_slot,) + local_grads.shape[1:], jnp.float32)
        .at[assignment]
        .set(local_grads)
    )
    owned_full = lax.psum_scatter(
        padded_grads.astype(jnp.bfloat16), "dp", scatter_dimension=0, tiled=True
    )
    owned = lax.psum_scatter(owned_full, "space", scatter_dimension=2, tiled=True).astype(
        jnp.float32
    )
    new_first = 0.9 * moment_first + 0.1 * owned
    new_second = 0.999 * moment_second + 0.001 * owned * owned
    update = new_first / bias_one / (jnp.sqrt(new_second / bias_two) + epsilon)
    new_master = master_weights - learn_rate * (update + decay_rate * master_weights)
    mine_rounded = new_master.astype(jnp.bfloat16)
    gathered = lax.all_gather(mine_rounded, "dp", axis=0, tiled=True)
    picked = jnp.take(gathered, assignment, axis=0)
    new_params = lax.all_gather(picked, "space", axis=2, tiled=True)
    kernel_c = new_params[2].reshape(27, channels, channels)
    kernel_d = new_params[3].reshape(27, channels, channels)
    enc_field = encoder_input[0]
    first = forward_local(widened(enc_field), kernel_c)
    activ = (first * jax.nn.sigmoid(first)).astype(jnp.bfloat16).reshape(field_shape)
    second = forward_local(widened(activ), kernel_d)
    encoder_out = (enc_field.reshape(channels, -1).astype(jnp.float32) + second).astype(
        jnp.bfloat16
    )
    encoder_out = encoder_out.reshape((1,) + field_shape)
    return (input_grad, encoder_out, new_params, new_first, new_second, new_master)


def solution(mesh):
    in_specs = (
        P("dp", None, "space", None, None),
        P("dp", None, "space", None, None),
        P("dp", None, "space", None, None),
        P(),
        P("dp", "space", None, None, None),
        P(),
        P("dp", None, "space"),
        P("dp", None, "space"),
        P("dp", None, "space"),
    )
    out_specs = (
        P("dp", None, "space", None, None),
        P("dp", None, "space", None, None),
        P(),
        P("dp", None, "space"),
        P("dp", None, "space"),
        P("dp", None, "space"),
    )
    return jax.shard_map(
        per_device, mesh=mesh, in_specs=in_specs, out_specs=out_specs, check_vma=False
    )
```

profile of v0, /device:TPU:0, one launch (start us, length us, event | category | flops | bytes accessed | tf_op | source)
XLA Modules:
  0.0 443.7 jit_solution(9299863268901218575)
XLA Ops:
  7.2 1.9 fusion.119
  9.1 2.9 collective-permute-start
  18.1 6.1 %fusion.104 = (f32[1,1,12,27,4096]{4,3,2,1,0:T(8,128)}, f32[12,27,4096]{2,1,0:T(8,128)}) fusion(bf16[1,1,12,27,4096]{4,3,2,1,0:T(8,128)(2,1)S(1)} %copy-done.10), kind=kLoop, calls=%fused_computation.149 | loop fusion | flops 1327104 | bytes 13271040 | tf_op jit(solution)/shard_map/convert_element_type | solution.py:112
  28.5 2.5 copy.138
  33.0 5.4 %maximum_bitcast_fusion = bf16[64,4,18,1,130]{4,2,1,0,3:T(8,128)(2,1)} fusion(bf16[64,4,18,1]{3,2,1,0:T(8,128)(2,1)S(1)} %get-tuple-element.67, bf16[64,4,1,128]{3,2,1,0:T(2,128)(2,1)S(1)} %get-tuple-element.89, bf16[64,1,16,128]{3,2,1,0:T(8,128)(2,1)S(1)} %collective-permute-done.1, bf16[64,2,16,128]{3,2,1,0:T(8,128)(2,1)S(1)} %bitcast.163, ...), kind=kLoop, calls=%fused_computation.8 | loop fusion | flops 8386560 | bytes 2396160 | tf_op jit(solution)/shard_map/broadcast_in_dim | solution.py:54
  38.4 7.9 %copy.160 = bf16[64,4,18,1,130]{0,1,4,2,3:T(4,128)(2,1)S(1)} copy(bf16[64,4,18,1,130]{4,2,1,0,3:T(8,128)(2,1)} %maximum_bitcast_fusion) | data formatting | bytes 2396160
  48.6 4.3 fusion.53
  53.5 2.2 copy.157
  56.6 3.7 fusion.132
  60.2 6.1 %copy.161 = bf16[64,4,18,1,130]{0,1,4,2,3:T(4,128)(2,1)} copy(bf16[64,4,18,1,130]{4,0,2,1,3:T(8,128)(2,1)} %fusion.132) | data formatting | bytes 2396160
  66.3 2.9 pad.6.clone
  70.3 8.6 %fusion.50 = f32[2,16,8,17,64]{4,2,3,1,0:T(8,128)S(1)} fusion(bf16[3,3,3,64,64]{4,3,2,1,0:T(8,128)(2,1)S(1)} %copy-done.19, bf16[64,4,18,1,7,2]{0,4,5,2,1,3:T(8,128)(2,1)S(1)} %slice.233, bf16[64,4,18,1,8,17]{0,4,5,2,1,3:T(8,128)(2,1)S(1)} %copy.115, pred[8,17]{0,1:T(8,128)(4,1)S(1)} %copy-done.27), kind=kOutput, calls=%fused_computation.54 | convolution fusion | flops 967073792 | bytes 2717832 | tf_op jit(solution)/shard_map/conv_general_dilated | solution.py:39
  80.8 3.7 copy.158
  84.5 2.2 fusion.76
  89.3 2.4 collective-permute-start.9
  91.7 4.4 copy.132
  96.1 4.6 %fusion.131 = bf16[1,64,4,18,130]{4,1,3,2,0:T(8,128)(2,1)} fusion(bf16[64,4,18,1]{3,0,2,1:T(8,128)(2,1)S(1)} %get-tuple-element.75, bf16[64,4,1,128]{3,0,2,1:T(8,128)(2,1)} %copy-done.14, bf16[64,1,16,128]{3,0,2,1:T(8,128)(2,1)} %copy-done.8, bf16[64,2,16,128]{3,0,2,1:T(8,128)(2,1)S(1)} %bitcast.158, bf16[64,1,16,128]{3,0,2,1:T(8,128)(2,1)} %copy-done.7, ...), kind=kLoop, calls=%fused_computation.167 | loop fusion | flops 8386560 | bytes 2396160 | tf_op jit(solution)/shard_map/broadcast_in_dim | solution.py:40
  100.7 12.3 %copy.131 = bf16[1,64,4,18,130]{1,0,4,3,2:T(2,128)(2,1)} copy(bf16[1,64,4,18,130]{4,1,3,2,0:T(8,128)(2,1)} %fusion.131) | data formatting | bytes 2396160 | tf_op jit(solution)/shard_map/broadcast_in_dim | solution.py:40
  113.0 33.5 %fusion.120 = f32[3,3,3,64,64]{4,3,2,1,0:T(8,128)} fusion(bf16[1,64,4,18,130]{1,0,4,3,2:T(2,128)(2,1)} %copy.131, bf16[64,1,2,16,128]{0,1,4,3,2:T(2,128)(2,1)S(1)} %copy-done.12), kind=kOutput, calls=%fused_computation.165 | convolution fusion | flops 905969664 | bytes 2164736 | tf_op jit(solution)/shard_map/transpose | solution.py:74
  148.0 1.9 fusion.80
  154.0 9.2 %copy.137 = bf16[1,64,4,18,130]{1,0,4,3,2:T(2,128)(2,1)} copy(bf16[1,64,4,18,130]{4,1,3,2,0:T(8,128)(2,1)S(1)} %maximum_bitcast_fusion.3) | data formatting | bytes 2396160 | tf_op jit(solution)/shard_map/broadcast_in_dim | solution.py:67
  163.1 32.5 %fusion.121 = f32[3,3,3,64,64]{4,3,2,1,0:T(8,128)S(1)} fusion(bf16[1,64,4,18,130]{1,0,4,3,2:T(2,128)(2,1)} %copy.137, bf16[64,1,2,16,128]{0,1,4,3,2:T(2,128)(2,1)} %copy.138), kind=kOutput, calls=%fused_computation.166 | convolution fusion | flops 905969664 | bytes 2164736 | tf_op jit(solution)/shard_map/transpose | solution.py:74
  195.9 1.9 fusion.78
  197.8 6.4 %broadcast_multiply_fusion = f32[12,27,4096]{2,1,0:T(8,128)} fusion(f32[12,27,4096]{2,1,0:T(8,128)} %fusion.78), kind=kLoop, calls=%fused_computation.10 | loop fusion | flops 1327104 | bytes 10616832 | tf_op jit(solution)/shard_map/mul | solution.py:115
  204.2 4.3 broadcast_in_dim.40
  208.5 11.7 %scatter_fusion = f32[16,27,4096]{2,1,0:T(8,128)} fusion(f32[16,27,4096]{2,1,0:T(8,128)} %broadcast_in_dim.40, s32[12]{0:T(128)S(1)} %compare_select_fusion, f32[12,27,4096]{2,1,0:T(8,128)} %broadcast_multiply_fusion), kind=kCustom, calls=%fused_computation.1 | custom fusion | bytes 15925296 | tf_op jit(solution)/shard_map/scatter | solution.py:121
  220.2 6.1 %convert_element_type.55 = bf16[16,27,4096]{2,1,0:T(8,128)(2,1)} convert(f32[16,27,4096]{2,1,0:T(8,128)} %scatter_fusion) | non-fusion elementwise | flops 1769472 | bytes 10616832 | tf_op jit(solution)/shard_map/convert_element_type | solution.py:124
  226.4 50.9 %reduce-scatter.3.cloned.1.call-done = bf16[2,27,4096]{2,1,0:T(8,128)(2,1)} async-done(((bf16[16,27,4096]{2,1,0:T(8,128)(2,1)}), bf16[2,27,4096]{2,1,0:T(8,128)(2,1)}) %reduce-scatter.3.cloned.1.call-update) | async-done | bytes 442384 | tf_op jit(solution)/shard_map/reduce_scatter | solution.py:123
  277.4 25.7 %reduce-scatter.5.cloned.1.call-done = bf16[2,27,1024]{2,1,0:T(8,128)(2,1)} async-done(((bf16[2,27,4096]{2,1,0:T(8,128)(2,1)}), bf16[2,27,1024]{2,1,0:T(8,128)(2,1)}) %reduce-scatter.5.cloned.1.call-update) | async-done | bytes 110608 | tf_op jit(solution)/shard_map/reduce_scatter | solution.py:126
  303.1 2.1 fusion.100
  305.3 16.5 %all_gather.6 = bf16[16,27,1024]{2,1,0:T(8,128)(2,1)S(1)} all-gather(bf16[2,27,1024]{2,1,0:T(8,128)(2,1)S(1)} %get-tuple-element.56), channel_id=1, replica_groups=mesh['dp'=8,'space'=4] {'dp'}, dimensions={0}, use_global_device_ids=true | all-gather | bytes 995328 | tf_op jit(solution)/shard_map/all_gather | solution.py:134
  326.5 2.2 copy.125
  329.9 2.4 collective-permute-start.5
  333.6 10.1 %collective-permute-done.7 = bf16[64,1,16,128]{3,2,1,0:T(8,128)(2,1)S(1)} collective-permute-done((bf16[64,1,16,128]{3,2,1,0:T(8,128)(2,1)S(1)}, bf16[64,1,16,128]{3,2,1,0:T(8,128)(2,1)S(1)}, u32[]{:S(2)}, u32[]{:S(2)}) %collective-permute-start.7) | collective-permute-done | bytes 262176 | tf_op jit(solution)/shard_map/ppermute | solution.py:26
  345.6 5.4 %maximum_bitcast_fusion.1 = bf16[64,4,18,1,130]{4,2,1,0,3:T(8,128)(2,1)} fusion(bf16[64,4,18,1]{3,2,1,0:T(8,128)(2,1)S(1)} %get-tuple-element.65, bf16[64,4,1,128]{3,2,1,0:T(2,128)(2,1)S(1)} %get-tuple-element.79, bf16[64,1,16,128]{3,2,1,0:T(8,128)(2,1)S(1)} %collective-permute-done.7, bf16[64,2,16,128]{3,2,1,0:T(8,128)(2,1)S(1)} %bitcast.167, ...), kind=kLoop, calls=%fused_computation.9 | loop fusion | flops 8386560 | bytes 2396160 | tf_op jit(solution)/shard_map/broadcast_in_dim | solution.py:40
  350.9 7.9 %copy.162 = bf16[64,4,18,1,130]{0,1,4,2,3:T(4,128)(2,1)S(1)} copy(bf16[64,4,18,1,130]{4,2,1,0,3:T(8,128)(2,1)} %maximum_bitcast_fusion.1) | data formatting | bytes 2396160
  364.1 2.7 maximum_bitcast_fusion.2
  366.9 4.9 %copy.163 = bf16[64,4,18,1,130]{0,1,4,2,3:T(4,128)(2,1)S(1)} copy(bf16[64,4,18,1,130]{4,0,2,1,3:T(8,128)(2,1)} %maximum_bitcast_fusion.2) | data formatting | bytes 2396160
  374.1 4.3 select_convert_fusion
  380.8 10.5 %fusion.47 = f32[2,16,8,17,64]{4,2,3,1,0:T(8,128)S(1)} fusion(bf16[3,3,3,64,64]{4,3,2,1,0:T(8,128)(2,1)S(1)} %reshape_reshape_squeeze.15, bf16[64,4,18,1,7,2]{0,4,5,2,1,3:T(8,128)(2,1)S(1)} %copy-done.22, bf16[64,4,18,1,8,17]{0,4,5,2,1,3:T(8,128)(2,1)} %copy-done.11, pred[8,17]{0,1:T(8,128)(4,1)S(1)} %copy-done.27), kind=kOutput, calls=%fused_computation.53 | convolution fusion | flops 967073792 | bytes 2717832 | tf_op jit(solution)/shard_map/conv_general_dilated | solution.py:39
  392.0 2.2 copy.159
  396.5 2.9 collective-permute-start.11
  399.6 2.1 copy.152
  406.5 2.4 collective-permute-done.11
  411.7 2.7 maximum_bitcast_fusion.4
  414.4 4.7 %copy.164 = bf16[64,4,18,1,130]{0,1,4,2,3:T(4,128)(2,1)S(1)} copy(bf16[64,4,18,1,130]{4,0,2,1,3:T(8,128)(2,1)} %maximum_bitcast_fusion.4) | data formatting | bytes 2396160
  420.8 8.6 %fusion.42 = f32[2,16,8,17,64]{4,2,3,1,0:T(8,128)S(1)} fusion(bf16[3,3,3,64,64]{4,3,2,1,0:T(8,128)(2,1)S(1)} %reshape_reshape_squeeze.16, bf16[64,4,18,1,7,2]{0,4,5,2,1,3:T(8,128)(2,1)S(1)} %slice.264, bf16[64,4,18,1,8,17]{0,4,5,2,1,3:T(8,128)(2,1)S(1)} %copy.150, pred[8,17]{0,1:T(8,128)(4,1)S(1)} %copy-done.27), kind=kOutput, calls=%fused_computation.52 | convolution fusion | flops 967073792 | bytes 2717832 | tf_op jit(solution)/shard_map/conv_general_dilated | solution.py:39
  431.8 3.4 copy.153
  (158 shorter events, 62.6 us)
Async XLA Ops:
  7.2 270.1 %reduce-scatter.3.cloned.1.call-start = ((), (), s32[]{:S(2)}) async-start(), calls=%async_computation.2 | async-start | bytes 4718592 | tf_op jit(solution)/shard_map/reduce_scatter | solution.py:123
  7.2 10.8 %copy-start.10 = (bf16[1,1,12,27,4096]{4,3,2,1,0:T(8,128)(2,1)S(1)}, bf16[1,1,12,27,4096]{4,3,2,1,0:T(8,128)(2,1)}, u32[]{:S(2)}) copy-start(bf16[1,1,12,27,4096]{4,3,2,1,0:T(8,128)(2,1)} %param.17) | copy-start | bytes 7962628
  9.1 21.9 %collective-permute-start = (bf16[64,1,16,128]{3,2,1,0:T(8,128)(2,1)}, bf16[64,1,16,128]{3,2,1,0:T(8,128)(2,1)S(1)}, u32[]{:S(2)}, u32[]{:S(2)}) collective-permute-start(bf16[64,1,16,128]{3,2,1,0:T(8,128)(2,1)} %get-tuple-element.100), channel_id=1, source_target_pairs={{0,1},{1,2},{2,3},{3,0},{4,5},{5,6},{6,7},{7,4},{8,9},{9,10},{10,1... | collective-permute-start | bytes 786440 | tf_op jit(solution)/shard_map/ppermute | solution.py:23
  12.1 19.0 %collective-permute-start.1 = (bf16[64,1,16,128]{3,2,1,0:T(8,128)(2,1)S(1)}, bf16[64,1,16,128]{3,2,1,0:T(8,128)(2,1)S(1)}, u32[]{:S(2)}, u32[]{:S(2)}) collective-permute-start(bf16[64,1,16,128]{3,2,1,0:T(8,128)(2,1)S(1)} %get-tuple-element.101), channel_id=1, source_target_pairs={{1,0},{2,1},{3,2},{0,3},{5,4},{6,5},{7,6},{4,7},{9,8},{10,9},{11,1... | collective-permute-start | bytes 786440 | tf_op jit(solution)/shard_map/ppermute | solution.py:26
  15.1 40.6 %collective-permute-start.2 = (bf16[64,1,16,128]{3,0,2,1:T(8,128)(2,1)}, bf16[64,1,16,128]{3,0,2,1:T(8,128)(2,1)S(1)}, u32[]{:S(2)}, u32[]{:S(2)}) collective-permute-start(bf16[64,1,16,128]{3,0,2,1:T(8,128)(2,1)} %get-tuple-element.98), channel_id=1, source_target_pairs={{0,1},{1,2},{2,3},{3,0},{4,5},{5,6},{6,7},{7,4},{8,9},{9,10},{10,1... | collective-permute-start | bytes 786440 | tf_op jit(solution)/shard_map/ppermute | solution.py:23
  16.2 8.0 %copy-start.13 = (bf16[2,27,4096]{2,0,1:T(2,128)(2,1)S(1)}, bf16[2,27,4096]{2,0,1:T(2,128)(2,1)}, u32[]{:S(2)}) copy-start(bf16[2,27,4096]{2,0,1:T(2,128)(2,1)} %param.16) | copy-start | bytes 1327108
  16.2 39.5 %collective-permute-start.3 = (bf16[64,1,16,128]{3,0,2,1:T(8,128)(2,1)}, bf16[64,1,16,128]{3,0,2,1:T(8,128)(2,1)S(1)}, u32[]{:S(2)}, u32[]{:S(2)}) collective-permute-start(bf16[64,1,16,128]{3,0,2,1:T(8,128)(2,1)} %get-tuple-element.99), channel_id=1, source_target_pairs={{1,0},{2,1},{3,2},{0,3},{5,4},{6,5},{7,6},{4,7},{9,8},{10,9},{11,1... | collective-permute-start | bytes 786440 | tf_op jit(solution)/shard_map/ppermute | solution.py:26
  24.2 4.3 copy-start
  24.2 6.9 %copy-start.26 = (s32[12]{0:T(128)S(1)}, s32[12]{0:T(128)}, u32[]{:S(2)}) copy-start(s32[12]{0:T(128)} %param.18) | copy-start | bytes 148
  47.6 1.0 copy-start.21
  47.6 1.0 copy-start.27
  55.7 0.8 copy-start.7
  55.7 0.8 copy-start.8
  55.8 0.8 copy-start.14
  69.3 1.0 copy-start.19
  84.5 2.2 copy-start.2
  84.5 2.2 copy-start.3
  86.7 1.2 copy-start.4
  88.8 61.1 %collective-permute-start.8 = (bf16[64,1,16,128]{3,2,1,0:T(8,128)(2,1)}, bf16[64,1,16,128]{3,2,1,0:T(8,128)(2,1)}, u32[]{:S(2)}, u32[]{:S(2)}) collective-permute-start(bf16[64,1,16,128]{3,2,1,0:T(8,128)(2,1)} %get-tuple-element.94), channel_id=1, source_target_pairs={{0,1},{1,2},{2,3},{3,0},{4,5},{5,6},{6,7},{7,4},{8,9},{9,10},{10,1... | collective-permute-start | bytes 786440 | tf_op jit(solution)/shard_map/ppermute | solution.py:23
  89.3 60.6 %collective-permute-start.9 = (bf16[64,1,16,128]{3,2,1,0:T(8,128)(2,1)}, bf16[64,1,16,128]{3,2,1,0:T(8,128)(2,1)}, u32[]{:S(2)}, u32[]{:S(2)}) collective-permute-start(bf16[64,1,16,128]{3,2,1,0:T(8,128)(2,1)} %get-tuple-element.95), channel_id=1, source_target_pairs={{1,0},{2,1},{3,2},{0,3},{5,4},{6,5},{7,6},{4,7},{9,8},{10,9},{11,1... | collective-permute-start | bytes 786440 | tf_op jit(solution)/shard_map/ppermute | solution.py:26
  100.6 12.3 %copy-start.12 = (bf16[64,1,2,16,128]{0,1,4,3,2:T(2,128)(2,1)S(1)}, bf16[64,1,2,16,128]{0,1,4,3,2:T(2,128)(2,1)}, u32[]{:S(2)}) copy-start(bf16[64,1,2,16,128]{0,1,4,3,2:T(2,128)(2,1)} %copy.132) | copy-start | bytes 1572868
  146.4 3.5 copy-start.5
  226.3 76.8 %copy-start.23 = (f32[2,27,1024]{2,0,1:T(2,128)S(1)}, f32[2,27,1024]{2,0,1:T(2,128)}, u32[]{:S(2)}) copy-start(f32[2,27,1024]{2,0,1:T(2,128)} %param.21) | copy-start | bytes 663556
  226.3 76.8 %copy-start.24 = (f32[2,27,1024]{2,0,1:T(2,128)S(1)}, f32[2,27,1024]{2,0,1:T(2,128)}, u32[]{:S(2)}) copy-start(f32[2,27,1024]{2,0,1:T(2,128)} %param.19) | copy-start | bytes 663556
  226.3 76.8 %copy-start.25 = (f32[2,27,1024]{2,0,1:T(2,128)S(1)}, f32[2,27,1024]{2,0,1:T(2,128)}, u32[]{:S(2)}) copy-start(f32[2,27,1024]{2,0,1:T(2,128)} %param.20) | copy-start | bytes 663556
  226.3 76.8 %reduce-scatter.5.cloned.1.call-start = ((), (), s32[]{:S(2)}) async-start(), calls=%async_computation.3 | async-start | bytes 655360 | tf_op jit(solution)/shard_map/reduce_scatter | solution.py:126
  277.3 101.3 %all-gather.2.cloned.1.call-start = ((), (), s32[]{:S(2)}) async-start(), calls=%async_computation.4 | async-start | bytes 3932160 | tf_op jit(solution)/shard_map/all_gather | solution.py:136
  305.3 18.2 %copy-start.1 = (bf16[1,64,2,16,128]{4,3,2,1,0:T(8,128)(2,1)S(1)}, bf16[1,64,2,16,128]{4,3,2,1,0:T(8,128)(2,1)}, u32[]{:S(2)}) copy-start(bf16[1,64,2,16,128]{4,3,2,1,0:T(8,128)(2,1)} %param.15) | copy-start | bytes 1572868
  323.5 10.1 %collective-permute-start.6 = (bf16[64,1,16,128]{3,2,1,0:T(8,128)(2,1)S(1)}, bf16[64,1,16,128]{3,2,1,0:T(8,128)(2,1)S(1)}, u32[]{:S(2)}, u32[]{:S(2)}) collective-permute-start(bf16[64,1,16,128]{3,2,1,0:T(8,128)(2,1)S(1)} %get-tuple-element.92), channel_id=1, source_target_pairs={{0,1},{1,2},{2,3},{3,0},{4,5},{5,6},{6,7},{7,4},{8,9},{9,10},{10,1... | collective-permute-start | bytes 786440 | tf_op jit(solution)/shard_map/ppermute | solution.py:23
  325.0 18.7 %collective-permute-start.7 = (bf16[64,1,16,128]{3,2,1,0:T(8,128)(2,1)S(1)}, bf16[64,1,16,128]{3,2,1,0:T(8,128)(2,1)S(1)}, u32[]{:S(2)}, u32[]{:S(2)}) collective-permute-start(bf16[64,1,16,128]{3,2,1,0:T(8,128)(2,1)S(1)} %get-tuple-element.93), channel_id=1, source_target_pairs={{1,0},{2,1},{3,2},{0,3},{5,4},{6,5},{7,6},{4,7},{9,8},{10,9},{11,1... | collective-permute-start | bytes 786440 | tf_op jit(solution)/shard_map/ppermute | solution.py:26
  329.3 32.0 %collective-permute-start.4 = (bf16[64,1,16,128]{3,2,1,0:T(8,128)(2,1)}, bf16[64,1,16,128]{3,2,1,0:T(8,128)(2,1)}, u32[]{:S(2)}, u32[]{:S(2)}) collective-permute-start(bf16[64,1,16,128]{3,2,1,0:T(8,128)(2,1)} %get-tuple-element.96), channel_id=1, source_target_pairs={{0,1},{1,2},{2,3},{3,0},{4,5},{5,6},{6,7},{7,4},{8,9},{9,10},{10,1... | collective-permute-start | bytes 786440 | tf_op jit(solution)/shard_map/ppermute | solution.py:23
  329.9 31.5 %collective-permute-start.5 = (bf16[64,1,16,128]{3,2,1,0:T(8,128)(2,1)S(1)}, bf16[64,1,16,128]{3,2,1,0:T(8,128)(2,1)}, u32[]{:S(2)}, u32[]{:S(2)}) collective-permute-start(bf16[64,1,16,128]{3,2,1,0:T(8,128)(2,1)S(1)} %get-tuple-element.97), channel_id=1, source_target_pairs={{1,0},{2,1},{3,2},{0,3},{5,4},{6,5},{7,6},{4,7},{9,8},{10,9},{11,1... | collective-permute-start | bytes 786440 | tf_op jit(solution)/shard_map/ppermute | solution.py:26
  360.5 2.3 copy-start.11
  373.1 1.0 copy-start.20
  378.4 2.4 copy-start.22
  395.6 6.1 %copy-start.17 = (f32[2,27,1024]{2,1,0:T(8,128)S(1)}, f32[2,27,1024]{2,1,0:T(8,128)}, u32[]{:S(2)}) copy-start(f32[2,27,1024]{2,1,0:T(8,128)} %get-tuple-element.58) | copy-start | bytes 663556
  395.7 6.9 %copy-start.16 = (f32[2,27,1024]{2,1,0:T(8,128)S(1)}, f32[2,27,1024]{2,1,0:T(8,128)}, u32[]{:S(2)}) copy-start(f32[2,27,1024]{2,1,0:T(8,128)} %get-tuple-element.59) | copy-start | bytes 663556
  396.5 6.9 %copy-start.15 = (f32[2,27,1024]{2,1,0:T(8,128)S(1)}, f32[2,27,1024]{2,1,0:T(8,128)}, u32[]{:S(2)}) copy-start(f32[2,27,1024]{2,1,0:T(8,128)} %get-tuple-element.57) | copy-start | bytes 663556
  396.5 10.0 %collective-permute-start.10 = (bf16[64,1,16,128]{3,2,1,0:T(8,128)(2,1)}, bf16[64,1,16,128]{3,2,1,0:T(8,128)(2,1)}, u32[]{:S(2)}, u32[]{:S(2)}) collective-permute-start(bf16[64,1,16,128]{3,2,1,0:T(8,128)(2,1)} %get-tuple-element.90), channel_id=1, source_target_pairs={{0,1},{1,2},{2,3},{3,0},{4,5},{5,6},{6,7},{7,4},{8,9},{9,10},{10,1... | collective-permute-start | bytes 786440 | tf_op jit(solution)/shard_map/ppermute | solution.py:23
  396.5 12.5 %collective-permute-start.11 = (bf16[64,1,16,128]{3,2,1,0:T(8,128)(2,1)}, bf16[64,1,16,128]{3,2,1,0:T(8,128)(2,1)}, u32[]{:S(2)}, u32[]{:S(2)}) collective-permute-start(bf16[64,1,16,128]{3,2,1,0:T(8,128)(2,1)} %get-tuple-element.91), channel_id=1, source_target_pairs={{1,0},{2,1},{3,2},{0,3},{5,4},{6,5},{7,6},{4,7},{9,8},{10,9},{11,1... | collective-permute-start | bytes 786440 | tf_op jit(solution)/shard_map/ppermute | solution.py:26
  399.6 4.7 %copy-start.18 = (bf16[1,27,4096]{2,1,0:T(8,128)(2,1)S(1)}, bf16[1,27,4096]{2,1,0:T(8,128)(2,1)}, u32[]{:S(2)}) copy-start(bf16[1,27,4096]{2,1,0:T(8,128)(2,1)} %get-tuple-element.61) | copy-start | bytes 663556
  429.4 1.2 copy-start.9
  430.6 4.6 %copy-start.6 = (bf16[12,27,4096]{2,1,0:T(8,128)(2,1)S(1)}, bf16[12,27,4096]{2,1,0:T(8,128)(2,1)}, u32[]{:S(2)}) copy-start(bf16[12,27,4096]{2,1,0:T(8,128)(2,1)} %all-gather.2.cloned.1.call-done) | copy-start | bytes 7962628
Sparse Core Ops, SparseCore 0:
  226.5 50.7 reduce-scatter.2
  280.1 22.9 reduce-scatter.4
  323.5 52.6 all-gather.1
where the time goes:
time: 452 us; the launch traced here: 444 us
  local copies, waits for them, and re-layouts  136 us (30%)
  matrix products  102 us (23%)
  waiting for transfers between devices  92.2 us (20%)
  other arithmetic  63.6 us (14%)
  starting transfers between devices  18.7 us (4%)
  blocking collectives  16.5 us (4%)
  between operations  14.7 us (3%)
    transpose x2, matrix products, kernel_grad(): return result.transpose(2, 3, 4, 1, 0).reshape(27, channels, channels)  65.9 us
    unnamed x78, local copies, waits for them, and re-layouts  57.7 us
    reduce_scatter x1, waiting for transfers between devices, per_device(): lax.psum_scatter(padded_grads.astype(jnp.bfloat16), 'dp', scatter_dimensi...  50.9 us
    conv_general_dilated x3, matrix products, forward_local(): lax.conv_general_dilated(padded[None], weights, (1, 1, 1), 'VALID', dimen...  27.7 us
    reduce_scatter x1, waiting for transfers between devices, per_device(): lax.psum_scatter(owned_full, 'space', scatter_dimension=2, tiled=True)  25.7 us
    broadcast_in_dim x4, local copies, waits for them, and re-layouts, forward_local(): padded[None]  17.8 us
    all_gather x1, blocking collectives, per_device(): gathered = lax.all_gather(mine_rounded, 'dp', axis=0, tiled=True)  16.5 us
    broadcast_in_dim x4, other arithmetic, forward_local(): padded[None]  16.4 us
  transfers between devices with their start and end apart: 15, of which 6 were waited for; matrix products, arithmetic and copies ran while one was open for 31% of the time, Pallas kernels for 0%

commit v1 on v0

v1 whole, which is shorter than its diff:
```python
import functools
import math

import jax
import jax.numpy as jnp
from jax import lax
from jax.experimental import pallas as pl
from jax.experimental.pallas import tpu as pltpu
from jax.sharding import PartitionSpec as P

learn_rate = 0.002
decay_rate = 0.1
epsilon = 1e-08
bias_one = 1.0 - (0.9**50) ** 2
bias_two = 1.0 - (0.999**50) ** 2

TILE = 512
LANES = 128


def rolled(tile, shift):
    groups = tile.shape[1] // LANES
    return jnp.concatenate(
        [pltpu.roll(tile[:, g * LANES : (g + 1) * LANES], shift, 1) for g in range(groups)], axis=1
    )


def stack_planes(target, refs, rows):
    channels = refs[0].shape[2]
    for number, ref in enumerate(refs):
        for x in range(ref.shape[0]):
            plane = number * ref.shape[0] + x

            def row(y, _, ref=ref, x=x, plane=plane):
                value = ref[x, y]
                for b in range(3):
                    at = plane * rows + lax.rem(y + 1 - b + rows, rows)
                    at = pl.multiple_of(at * LANES, LANES)
                    target[b * channels : (b + 1) * channels, pl.ds(at, LANES)] = value
                return 0

            lax.fori_loop(0, rows, row, 0)


def stack_tile(target, tile, n, rows):
    channels = tile.shape[0]
    per = tile.shape[1] // LANES
    for g in range(per):
        r = n * per + g
        plane, y = r // rows, lax.rem(r, rows)
        for b in range(3):
            at = plane * rows + lax.rem(y + 1 - b + rows, rows)
            at = pl.multiple_of(at * LANES, LANES)
            target[b * channels : (b + 1) * channels, pl.ds(at, LANES)] = tile[
                :, g * LANES : (g + 1) * LANES
            ]


def conv_tile(weights, stacked, n, cells, first_plane=0):
    channels = weights.shape[1] // 3
    total = None
    for a in range(3):
        at = pl.multiple_of(n * TILE + (a + first_plane) * cells, TILE)
        part = jnp.dot(
            weights[a], stacked[:, pl.ds(at, TILE)], preferred_element_type=jnp.float32
        )
        total = part if total is None else total + part
    return (
        total[channels : 2 * channels]
        + rolled(total[:channels], 1)
        + rolled(total[2 * channels :], LANES - 1)
    )


def store_rows(out_ref, tile, n, rows):
    per = tile.shape[1] // LANES
    for g in range(per):
        r = n * per + g
        out_ref[r // rows, lax.rem(r, rows)] = tile[:, g * LANES : (g + 1) * LANES]


def shifted_stack(target, n, tile):
    channels = tile.shape[0]
    at = pl.ds(pl.multiple_of(n * TILE, TILE), TILE)
    wide = tile.astype(jnp.float32)
    target[:channels, at] = rolled(wide, LANES - 1).astype(jnp.bfloat16)
    target[channels : 2 * channels, at] = tile
    target[2 * channels :, at] = rolled(wide, 1).astype(jnp.bfloat16)


def decoder_kernel(
    rows,
    dec_low, dec_mid, dec_high, cot_low, cot_mid, cot_high, w_a, w_bt, w_at,
    out_grad, out_a, out_b,
    f_dec, f_cot, f_hid, f_pre, s_cot, s_pre,
):
    thick = dec_mid.shape[0]
    cells = rows * LANES
    channels = dec_mid.shape[2]
    stack_planes(f_dec, (dec_low, dec_mid, dec_high), rows)
    stack_planes(f_cot, (cot_low, cot_mid, cot_high), rows)
    skip = thick - 1
    per_plane = cells // TILE

    def first(n, _):
        preact = conv_tile(w_a, f_dec, n, cells, skip - 1)
        grad_hidden = conv_tile(w_bt, f_cot, n, cells, skip - 1)
        sigma = jax.nn.sigmoid(preact)
        stack_tile(f_hid, (preact * sigma).astype(jnp.bfloat16), n, rows)
        grad_pre = grad_hidden * sigma * (1.0 + preact * (1.0 - sigma))
        stack_tile(f_pre, grad_pre.astype(jnp.bfloat16), n, rows)
        return 0

    lax.fori_loop(0, (thick + 2) * per_plane, first, 0)
    out_a[...] = jnp.zeros_like(out_a)
    out_b[...] = jnp.zeros_like(out_b)
    nt = (((1,), (1,)), ((), ()))

    def second(n, _):
        at = pl.ds(pl.multiple_of(n * TILE + cells, TILE), TILE)
        shifted_stack(s_pre, n, f_pre[channels : 2 * channels, at])
        at = pl.ds(pl.multiple_of(n * TILE + thick * cells, TILE), TILE)
        shifted_stack(s_cot, n, f_cot[channels : 2 * channels, at])
        here = pl.ds(pl.multiple_of(n * TILE, TILE), TILE)
        for a in range(3):
            at = pl.ds(pl.multiple_of(n * TILE + a * cells, TILE), TILE)
            out_b[a] += lax.dot_general(
                s_cot[:, here], f_hid[:, at], nt, preferred_element_type=jnp.float32
            )
            at = pl.ds(pl.multiple_of(n * TILE + (a + thick - 1) * cells, TILE), TILE)
            out_a[a] += lax.dot_general(
                s_pre[:, here], f_dec[:, at], nt, preferred_element_type=jnp.float32
            )
        tile = conv_tile(w_at, f_pre, n, cells)
        store_rows(out_grad, tile.astype(jnp.bfloat16), n, rows)
        return 0

    lax.fori_loop(0, thick * per_plane, second, 0)


def encoder_kernel(rows, low, mid, high, w_c, w_d, out, f_enc, f_act):
    thick = mid.shape[0]
    cells = rows * LANES
    channels = mid.shape[2]
    stack_planes(f_enc, (low, mid, high), rows)
    skip = thick - 1
    per_plane = cells // TILE

    def first(n, _):
        value = conv_tile(w_c, f_enc, n, cells, skip - 1)
        stack_tile(f_act, (value * jax.nn.sigmoid(value)).astype(jnp.bfloat16), n, rows)
        return 0

    lax.fori_loop(0, (thick + 2) * per_plane, first, 0)

    def second(n, _):
        value = conv_tile(w_d, f_act, n, cells)
        at = pl.ds(pl.multiple_of(n * TILE + thick * cells, TILE), TILE)
        base = f_enc[channels : 2 * channels, at].astype(jnp.float32)
        store_rows(out, (base + value).astype(jnp.bfloat16), n, rows)
        return 0

    lax.fori_loop(0, thick * per_plane, second, 0)


def whole(count):
    return [pl.BlockSpec(memory_space=pltpu.VMEM)] * count


def stacked_weights(kernel, channels):
    taps = kernel.reshape(3, 3, 3, channels, channels)
    return taps.transpose(0, 2, 3, 1, 4).reshape(3, 3 * channels, 3 * channels)


def turned_weights(kernel, channels):
    taps = kernel.reshape(3, 3, 3, channels, channels)[::-1, ::-1, ::-1]
    return taps.transpose(0, 2, 4, 1, 3).reshape(3, 3 * channels, 3 * channels)


def unstacked(grad, channels):
    taps = grad.reshape(3, 3, channels, 3, channels).transpose(0, 3, 1, 2, 4)
    return taps.reshape(27, channels * channels)


def neighbours(field):
    count = lax.axis_size("space")
    forward = [(i, (i + 1) % count) for i in range(count)]
    backward = [(target, source) for source, target in forward]
    low = lax.ppermute(field, "space", forward)
    high = lax.ppermute(field, "space", backward)
    return low, field, high


def adamw(moment_first, moment_second, master_weights, grads):
    new_first = 0.9 * moment_first + 0.1 * grads
    new_second = 0.999 * moment_second + 0.001 * grads * grads
    update = new_first / bias_one / (jnp.sqrt(new_second / bias_two) + epsilon)
    new_master = master_weights - learn_rate * (update + decay_rate * master_weights)
    return new_first, new_second, new_master


def per_device(
    decoder_input,
    cotangent,
    encoder_input,
    decoder_weights,
    other_grads,
    assignment,
    moment_first,
    moment_second,
    master_weights,
):
    channels, thick, rows, lanes = decoder_input.shape[1:]
    replicas = lax.axis_size("dp")
    slabs = lax.axis_size("space")
    slots, taps, share = moment_first.shape
    tensors = assignment.shape[0]
    every_slot = replicas * slots
    cells = rows * lanes
    scale = 1.0 / math.sqrt(replicas * thick * slabs * cells)
    params = pltpu.CompilerParams(vmem_limit_bytes=48 * 1024 * 1024)

    match = assignment[None, :] == jnp.arange(every_slot, dtype=jnp.int32)[:, None]
    used = jnp.any(match, axis=1)
    tensor_of = jnp.argmax(match, axis=1).astype(jnp.int32)
    by_slot = jnp.where(
        used[:, None, None], jnp.take(other_grads[0, 0], tensor_of, axis=0), 0
    ).astype(jnp.bfloat16)
    owned = lax.psum_scatter(by_slot, "dp", scatter_dimension=0, tiled=True)
    owned = lax.psum_scatter(owned, "space", scatter_dimension=2, tiled=True)
    owned = owned.astype(jnp.float32)

    dec = neighbours(decoder_input[0].transpose(1, 2, 0, 3))
    cot = neighbours(cotangent[0].transpose(1, 2, 0, 3))
    w_a = stacked_weights(decoder_weights[0], channels)
    w_at = turned_weights(decoder_weights[0], channels)
    w_bt = turned_weights(decoder_weights[1], channels)
    wide = 3 * channels
    field = jax.ShapeDtypeStruct((thick, rows, channels, lanes), jnp.bfloat16)
    small = jax.ShapeDtypeStruct((3, wide, wide), jnp.float32)
    bf = jnp.bfloat16
    conv_flops = 2 * 27 * channels * channels * cells
    input_grad, grad_a, grad_b = pl.pallas_call(
        functools.partial(decoder_kernel, rows),
        out_shape=(field, small, small),
        in_specs=whole(9),
        out_specs=tuple(whole(3)),
        scratch_shapes=[
            pltpu.VMEM((wide, 3 * thick * cells), bf),
            pltpu.VMEM((wide, 3 * thick * cells), bf),
            pltpu.VMEM((wide, (thick + 2) * cells), bf),
            pltpu.VMEM((wide, (thick + 2) * cells), bf),
            pltpu.VMEM((wide, thick * cells), bf),
            pltpu.VMEM((wide, thick * cells), bf),
        ],
        compiler_params=params,
        cost_estimate=pl.CostEstimate(
            flops=30 * conv_flops, bytes_accessed=8 * 2**20, transcendentals=0
        ),
        name="decoder",
    )(*dec, *cot, w_a, w_bt, w_at)
    input_grad = input_grad.transpose(2, 0, 1, 3)[None]

    pair = jnp.stack([unstacked(grad_a, channels), unstacked(grad_b, channels)])
    pair = lax.psum_scatter(pair.astype(bf), "space", scatter_dimension=2, tiled=True)
    pair = lax.psum(pair, "dp").astype(jnp.float32)

    mine = lax.axis_index("dp") * slots + jnp.arange(slots, dtype=jnp.int32)
    early = adamw(moment_first, moment_second, master_weights, owned * scale)[2]
    gathered = lax.all_gather(early.astype(bf), ("dp", "space"), axis=0)
    gathered = gathered.reshape(replicas, slabs, slots, taps, share)
    picked = gathered[assignment // slots, :, lax.rem(assignment, slots)]

    is_a = (mine == assignment[0])[:, None, None]
    is_b = (mine == assignment[1])[:, None, None]
    owned = owned + jnp.where(is_a, pair[0], 0.0) + jnp.where(is_b, pair[1], 0.0)
    new_first, new_second, new_master = adamw(
        moment_first, moment_second, master_weights, owned * scale
    )
    rounded = new_master.astype(bf)
    late = jnp.stack(
        [
            jnp.sum(jnp.where(is_a, rounded, 0), axis=0),
            jnp.sum(jnp.where(is_b, rounded, 0), axis=0),
        ]
    ).astype(bf)
    late = lax.psum(late, "dp")
    late = lax.all_gather(late, "space", axis=2, tiled=True)
    rest = picked[2:].transpose(0, 2, 1, 3).reshape(tensors - 2, taps, slabs * share)
    new_params = jnp.concatenate([late, rest], axis=0)

    enc = neighbours(encoder_input[0].transpose(1, 2, 0, 3))
    w_c = stacked_weights(rest[0], channels)
    w_d = stacked_weights(rest[1], channels)
    encoder_out = pl.pallas_call(
        functools.partial(encoder_kernel, rows),
        out_shape=field,
        in_specs=whole(5),
        out_specs=whole(1)[0],
        scratch_shapes=[
            pltpu.VMEM((wide, 3 * thick * cells), bf),
            pltpu.VMEM((wide, (thick + 2) * cells), bf),
        ],
        compiler_params=params,
        cost_estimate=pl.CostEstimate(
            flops=12 * conv_flops, bytes_accessed=4 * 2**20, transcendentals=0
        ),
        name="encoder",
    )(*enc, w_c, w_d)
    encoder_out = encoder_out.transpose(2, 0, 1, 3)[None]
    return (input_grad, encoder_out, new_params, new_first, new_second, new_master)


def solution(mesh):
    in_specs = (
        P("dp", None, "space", None, None),
        P("dp", None, "space", None, None),
        P("dp", None, "space", None, None),
        P(),
        P("dp", "space", None, None, None),
        P(),
        P("dp", None, "space"),
        P("dp", None, "space"),
        P("dp", None, "space"),
    )
    out_specs = (
        P("dp", None, "space", None, None),
        P("dp", None, "space", None, None),
        P(),
        P("dp", None, "space"),
        P("dp", None, "space"),
        P("dp", None, "space"),
    )
    return jax.shard_map(
        per_device, mesh=mesh, in_specs=in_specs, out_specs=out_specs, check_vma=False
    )
```

time: 452 us -> 438 us (0.969); the launches traced: 444 us -> 436 us
  waiting for transfers between devices: 92.2 us -> 257 us
  matrix products: 102 us -> 0 us
  other arithmetic: 63.6 us -> 17.9 us
  local copies, waits for them, and re-layouts: 136 us -> 91 us
  Pallas kernels: 0 us -> 33.3 us
  starting transfers between devices: 18.7 us -> 10 us
    psum x0 -> x2, waiting for transfers between devices: none -> 93.4 us  [the longest x1 52.9 us: per_device(): pair = lax.psum(pair, 'dp').astype(jnp.float32)]
    transpose x2 -> x0, matrix products: 65.9 us -> none  [kernel_grad(): return result.transpose(2, 3, 4, 1, 0).reshape(27, channels, channels)]
    all_gather x1, waiting for transfers between devices: 0.02 us -> 51.5 us  [per_device(): gathered = lax.all_gather(early.astype(bf), ('dp', 'space'), axis=0)]
    unnamed x78 -> x26, local copies, waits for them, and re-layouts: 57.7 us -> 18.5 us
    conv_general_dilated x5 -> x0, matrix products: 36.4 us -> none  [the longest x3 27.7 us: forward_local(): lax.conv_general_dilated(padded[None], weights, (1, 1, 1), 'VALID', dimen...]
    broadcast_in_dim x8 -> x0, local copies, waits for them, and re-layouts: 33.8 us -> none  [the longest x4 17.8 us: forward_local(): padded[None]]
    pallas_call x0 -> x2, Pallas kernels: none -> 33.3 us  [the longest x1 20.4 us: per_device(): pl.pallas_call(functools.partial(decoder_kernel, rows), out_shape=(field,...]
    broadcast_in_dim x7 -> x0, other arithmetic: 25.9 us -> none  [the longest x4 16.4 us: forward_local(): padded[None]]
  transfers between devices with their start and end apart: 15 -> 12, of which waited for: 6 -> 8; matrix products, arithmetic and copies ran while one was open for 31% -> 19% of each run, Pallas kernels for 0% -> 0%
where the time goes in v1:
time: 438 us; the launch traced here: 436 us
  waiting for transfers between devices  257 us (59%)
  local copies, waits for them, and re-layouts  91 us (21%)
  Pallas kernels  33.3 us (8%)
  other arithmetic  17.9 us (4%)
  between operations  14.3 us (3%)
  blocking collectives  12.3 us (3%)
  starting transfers between devices  10 us (2%)
    psum x1, waiting for transfers between devices, per_device(): pair = lax.psum(pair, 'dp').astype(jnp.float32)  52.9 us
    reduce_scatter x1, waiting for transfers between devices, per_device(): owned = lax.psum_scatter(by_slot, 'dp', scatter_dimension=0, tiled=True)  52.3 us
    all_gather x1, waiting for transfers between devices, per_device(): gathered = lax.all_gather(early.astype(bf), ('dp', 'space'), axis=0)  51.5 us
    psum x1, waiting for transfers between devices, per_device(): late = lax.psum(late, 'dp')  40.5 us
    reduce_scatter x1, waiting for transfers between devices, per_device(): owned = lax.psum_scatter(owned, 'space', scatter_dimension=2, tiled=True)  24.9 us
    reduce_scatter x1, waiting for transfers between devices, per_device(): lax.psum_scatter(pair.astype(bf), 'space', scatter_dimension=2, tiled=True)  20.5 us
    pallas_call x1, Pallas kernels, per_device(): pl.pallas_call(functools.partial(decoder_kernel, rows), out_shape=(field,...  20.4 us
    unnamed x26, local copies, waits for them, and re-layouts  18.5 us
  transfers between devices with their start and end apart: 12, of which 8 were waited for; matrix products, arithmetic and copies ran while one was open for 19% of the time, Pallas kernels for 0%

profile of v1, /device:TPU:0, one launch (start us, length us, event | category | flops | bytes accessed | tf_op | source)
XLA Modules:
  0.0 436.1 jit_solution(7561945713196944023)
XLA Ops:
  7.2 2.2 copy.138
  9.4 2.9 collective-permute-start
  13.3 2.0 copy.137
  16.4 1.9 collective-permute-start.3
  18.3 3.8 slice_reduce_fusion
  23.3 1.8 reverse_bitcast_fusion
  25.1 2.1 copy.91
  27.2 1.5 reshape.62.w_at
  28.7 2.2 copy.89
  30.9 2.2 reshape.60.w_a
  33.1 2.2 reshape_squeeze.14
  35.9 1.8 reverse_bitcast_fusion.1
  37.7 2.1 copy.90
  39.8 2.2 reshape.61.w_bt
  42.0 2.7 gather_fusion
  44.9 4.0 collective-permute-done.2.cot_low
  48.8 10.7 %collective-permute-done.3.cot_high = bf16[2,16,64,128]{3,2,1,0:T(8,128)(2,1)} collective-permute-done((bf16[2,16,64,128]{3,2,1,0:T(8,128)(2,1)}, bf16[2,16,64,128]{3,2,1,0:T(8,128)(2,1)}, u32[]{:S(2)}, u32[]{:S(2)}) %collective-permute-start.3) | collective-permute-done | bytes 524320 | tf_op jit(solution)/shard_map/ppermute | solution.py:190
  61.4 20.4 %decoder.1 = (bf16[2,16,64,128]{3,2,1,0:T(8,128)(2,1)S(1)}, f32[3,192,192]{2,1,0:T(8,128)S(1)}, f32[3,192,192]{2,1,0:T(8,128)S(1)}) custom-call(bf16[2,16,64,128]{3,2,1,0:T(8,128)(2,1)} %collective-permute-done.dec_low, bf16[2,16,64,128]{3,2,1,0:T(8,128)(2,1)} %bitcast.45.dec_mid, bf16[2,16,64,128]{3,2,1,0:T(8,128)(2,1)} %collective-permute-done.1.dec_high, ...), custom_call_target="tpu_custom_call" | custom-call | flops 13589544960 | bytes 8388608 | tf_op jit(solution)/shard_map/decoder/pallas_call | solution.py:243
  84.5 1.9 copy.101
  86.4 2.1 stack_reshape.8
  90.6 1.9 copy.102
  93.9 1.8 pad_maximum_fusion.1
  95.8 4.6 %select_select_fusion = bf16[16,27,4096]{2,1,0:T(8,128)(2,1)} fusion(bf16[16,27,4096]{2,1,0:T(8,128)(2,1)} %gather_fusion, pred[16]{0:T(512)(128)(4,1)S(1)} %compare_and_fusion, pred[16]{0:T(512)(128)(4,1)S(1)} %fusion.12), kind=kLoop, calls=%fused_computation.2 | loop fusion | flops 3538944 | bytes 7077920 | tf_op jit(solution)/shard_map/jit(_where)/select_n | solution.py:226
  100.5 20.5 %reduce-scatter.8.cloned.1.call-done = bf16[2,27,1024]{2,1,0:T(8,128)(2,1)} async-done(((bf16[2,27,4096]{2,1,0:T(8,128)(2,1)}), bf16[2,27,1024]{2,1,0:T(8,128)(2,1)}) %reduce-scatter.8.cloned.1.call-update) | async-done | bytes 110608 | tf_op jit(solution)/shard_map/reduce_scatter | solution.py:265
  121.1 52.3 %reduce-scatter.4.cloned.1.call-done = bf16[2,27,4096]{2,1,0:T(8,128)(2,1)} async-done(((bf16[16,27,4096]{2,1,0:T(8,128)(2,1)}), bf16[2,27,4096]{2,1,0:T(8,128)(2,1)}) %reduce-scatter.4.cloned.1.call-update) | async-done | bytes 442384 | tf_op jit(solution)/shard_map/reduce_scatter | solution.py:229
  175.4 52.9 %all-reduce.3.cloned.1.call-done = bf16[2,27,1024]{2,1,0:T(8,128)(2,1)} async-done(((bf16[2,27,1024]{2,1,0:T(8,128)(2,1)}), bf16[2,27,1024]{2,1,0:T(8,128)(2,1)}) %all-reduce.3.cloned.1.call-update) | async-done | bytes 110608 | tf_op jit(solution)/shard_map/psum | solution.py:266
  229.9 24.9 %reduce-scatter.6.cloned.1.call-done = bf16[2,27,1024]{2,1,0:T(8,128)(2,1)} async-done(((bf16[2,27,4096]{2,1,0:T(8,128)(2,1)}), bf16[2,27,1024]{2,1,0:T(8,128)(2,1)}) %reduce-scatter.6.cloned.1.call-update) | async-done | bytes 110608 | tf_op jit(solution)/shard_map/reduce_scatter | solution.py:230
  254.8 2.5 select_reduce_fusion.1
  258.0 2.2 fusion
  260.2 2.0 copy.136
  265.2 2.2 copy.104
  267.4 1.8 copy.106
  269.2 1.8 copy.107
  271.9 40.5 %all-reduce.5.cloned.1.call-done = bf16[2,27,1024]{2,1,0:T(8,128)(2,1)} async-done(((bf16[2,27,1024]{2,1,0:T(8,128)(2,1)}), bf16[2,27,1024]{2,1,0:T(8,128)(2,1)}) %all-reduce.5.cloned.1.call-update) | async-done | bytes 110608 | tf_op jit(solution)/shard_map/psum | solution.py:287
  312.3 12.3 %all_gather.11 = bf16[2,27,4096]{2,1,0:T(8,128)(2,1)} all-gather(bf16[2,27,1024]{2,1,0:T(8,128)(2,1)} %all-reduce.5.cloned.1.call-done), channel_id=1, replica_groups=mesh['dp'=8,'space'=4] {'space'}, dimensions={2}, use_global_device_ids=true | all-gather | bytes 552960 | tf_op jit(solution)/shard_map/all_gather | solution.py:288
  324.6 51.5 %all-gather.3.cloned.1.call-done = bf16[64,27,1024]{2,1,0:T(8,128)(2,1)} async-done(((bf16[2,27,1024]{2,1,0:T(8,128)(2,1)}), bf16[64,27,1024]{2,1,0:T(8,128)(2,1)}) %all-gather.3.cloned.1.call-update) | async-done | bytes 3538960 | tf_op jit(solution)/shard_map/all_gather | solution.py:270
  376.1 7.1 %copy.98 = bf16[8,4,2,27,1024]{4,1,3,2,0:T(4,128)(2,1)} copy(bf16[8,4,2,27,1024]{4,3,2,1,0:T(8,128)(2,1)} %bitcast.49) | data formatting | bytes 7077888 | tf_op jit(solution)/shard_map/reshape | solution.py:271
  383.2 6.9 %gather_fusion.1 = bf16[12,4,27,1024]{3,1,2,0:T(4,128)(2,1)} fusion(bf16[8,4,2,27,1024]{4,1,3,2,0:T(4,128)(2,1)} %copy.98, s32[12]{0:T(128)S(1)} %fusion.15), kind=kCustom, calls=%fused_computation.1 | custom fusion | bytes 5308512 | tf_op jit(solution)/shard_map/gather | solution.py:272
  390.1 3.8 slice_bitcast_fusion
  393.9 5.2 %reshape.68 = bf16[10,27,4096]{2,1,0:T(8,128)(2,1)} reshape(bf16[10,27,4,1024]{3,2,1,0:T(4,128)(2,1)} %slice_bitcast_fusion) | data formatting | bytes 4423680 | tf_op jit(solution)/shard_map/reshape | solution.py:289
  399.1 1.9 fusion.20
  402.0 2.2 copy.99
  404.2 1.5 reshape.64.w_c
  405.8 2.0 reshape_squeeze.16
  407.8 2.2 copy.100
  410.0 2.2 reshape.65.w_d
  413.2 12.9 %encoder.1 = bf16[2,16,64,128]{3,2,1,0:T(8,128)(2,1)S(1)} custom-call(bf16[2,16,64,128]{3,2,1,0:T(8,128)(2,1)} %collective-permute-done.4.low, bf16[2,16,64,128]{3,2,1,0:T(8,128)(2,1)} %bitcast.43.mid, bf16[2,16,64,128]{3,2,1,0:T(8,128)(2,1)} %collective-permute-done.5.high, bf16[3,192,192]{2,1,0:T(8,128)(2,1)S(1)} %reshape.64.w_c, ...), custom_call_target="tpu_custom_call" | custom-call | flops 5435817984 | bytes 4194304 | tf_op jit(solution)/shard_map/encoder/pallas_call | solution.py:295
  427.2 2.0 pad_maximum_fusion
  (58 shorter events, 23.5 us)
Async XLA Ops:
  7.2 34.8 %copy-start = (bf16[1,1,12,27,4096]{4,3,2,1,0:T(8,128)(2,1)S(1)}, bf16[1,1,12,27,4096]{4,3,2,1,0:T(8,128)(2,1)}, u32[]{:S(2)}) copy-start(bf16[1,1,12,27,4096]{4,3,2,1,0:T(8,128)(2,1)} %param.13) | copy-start | bytes 7962628
  7.2 113.8 %reduce-scatter.8.cloned.1.call-start = ((), (), s32[]{:S(2)}) async-start(), calls=%async_computation.5 | async-start | bytes 655360 | tf_op jit(solution)/shard_map/reduce_scatter | solution.py:265
  9.4 35.5 %collective-permute-start = (bf16[2,16,64,128]{3,2,1,0:T(8,128)(2,1)}, bf16[2,16,64,128]{3,2,1,0:T(8,128)(2,1)}, u32[]{:S(2)}, u32[]{:S(2)}) collective-permute-start(bf16[2,16,64,128]{3,2,1,0:T(8,128)(2,1)} %bitcast.45.dec_mid), channel_id=1, source_target_pairs={{0,1},{1,2},{2,3},{3,0},{4,5},{5,6},{6,7},{7,4},{8,9},{9,10},{10,1... | collective-permute-start | bytes 1572872 | tf_op jit(solution)/shard_map/ppermute | solution.py:189
  12.4 32.5 %collective-permute-start.1 = (bf16[2,16,64,128]{3,2,1,0:T(8,128)(2,1)}, bf16[2,16,64,128]{3,2,1,0:T(8,128)(2,1)}, u32[]{:S(2)}, u32[]{:S(2)}) collective-permute-start(bf16[2,16,64,128]{3,2,1,0:T(8,128)(2,1)} %bitcast.45.dec_mid), channel_id=1, source_target_pairs={{1,0},{2,1},{3,2},{0,3},{5,4},{6,5},{7,6},{4,7},{9,8},{10,9},{11,1... | collective-permute-start | bytes 1572872 | tf_op jit(solution)/shard_map/ppermute | solution.py:190
  15.4 33.5 %collective-permute-start.2 = (bf16[2,16,64,128]{3,2,1,0:T(8,128)(2,1)}, bf16[2,16,64,128]{3,2,1,0:T(8,128)(2,1)}, u32[]{:S(2)}, u32[]{:S(2)}) collective-permute-start(bf16[2,16,64,128]{3,2,1,0:T(8,128)(2,1)} %bitcast.44.cot_mid), channel_id=1, source_target_pairs={{0,1},{1,2},{2,3},{3,0},{4,5},{5,6},{6,7},{7,4},{8,9},{9,10},{10,1... | collective-permute-start | bytes 1572872 | tf_op jit(solution)/shard_map/ppermute | solution.py:189
  16.4 43.1 %collective-permute-start.3 = (bf16[2,16,64,128]{3,2,1,0:T(8,128)(2,1)}, bf16[2,16,64,128]{3,2,1,0:T(8,128)(2,1)}, u32[]{:S(2)}, u32[]{:S(2)}) collective-permute-start(bf16[2,16,64,128]{3,2,1,0:T(8,128)(2,1)} %bitcast.44.cot_mid), channel_id=1, source_target_pairs={{1,0},{2,1},{3,2},{0,3},{5,4},{6,5},{7,6},{4,7},{9,8},{10,9},{11,1... | collective-permute-start | bytes 1572872 | tf_op jit(solution)/shard_map/ppermute | solution.py:190
  22.0 13.2 %copy-start.8 = (s32[12]{0:T(128)S(1)}, s32[12]{0:T(128)}, u32[]{:S(2)}) copy-start(s32[12]{0:T(128)} %param.14) | copy-start | bytes 148
  59.5 1.0 copy-start.3
  60.5 1.0 copy-start.4
  81.8 0.8 copy-start.1
  82.7 0.8 copy-start.2
  95.7 77.7 %reduce-scatter.4.cloned.1.call-start = ((), (), s32[]{:S(2)}) async-start(), calls=%async_computation.3 | async-start | bytes 4718592 | tf_op jit(solution)/shard_map/reduce_scatter | solution.py:229
  100.5 127.8 %all-reduce.3.cloned.1.call-start = ((), (), s32[]{:S(2)}) async-start(), calls=%async_computation.6 | async-start | bytes 262144 | tf_op jit(solution)/shard_map/psum | solution.py:266
  121.0 133.7 %reduce-scatter.6.cloned.1.call-start = ((), (), s32[]{:S(2)}) async-start(), calls=%async_computation.4 | async-start | bytes 655360 | tf_op jit(solution)/shard_map/reduce_scatter | solution.py:230
  173.4 138.9 %all-reduce.5.cloned.1.call-start = ((), (), s32[]{:S(2)}) async-start(), calls=%async_computation.7 | async-start | bytes 262144 | tf_op jit(solution)/shard_map/psum | solution.py:287
  257.9 118.2 %all-gather.3.cloned.1.call-start = ((), (), s32[]{:S(2)}) async-start(), calls=%async_computation.8 | async-start | bytes 4325376 | tf_op jit(solution)/shard_map/all_gather | solution.py:270
  262.3 149.9 %collective-permute-start.4 = (bf16[2,16,64,128]{3,2,1,0:T(8,128)(2,1)}, bf16[2,16,64,128]{3,2,1,0:T(8,128)(2,1)}, u32[]{:S(2)}, u32[]{:S(2)}) collective-permute-start(bf16[2,16,64,128]{3,2,1,0:T(8,128)(2,1)} %bitcast.43.mid), channel_id=1, source_target_pairs={{0,1},{1,2},{2,3},{3,0},{4,5},{5,6},{6,7},{7,4},{8,9},{9,10},{10,1... | collective-permute-start | bytes 1572872 | tf_op jit(solution)/shard_map/ppermute | solution.py:189
  263.7 148.5 %collective-permute-start.5 = (bf16[2,16,64,128]{3,2,1,0:T(8,128)(2,1)}, bf16[2,16,64,128]{3,2,1,0:T(8,128)(2,1)}, u32[]{:S(2)}, u32[]{:S(2)}) collective-permute-start(bf16[2,16,64,128]{3,2,1,0:T(8,128)(2,1)} %bitcast.43.mid), channel_id=1, source_target_pairs={{1,0},{2,1},{3,2},{0,3},{5,4},{6,5},{7,6},{4,7},{9,8},{10,9},{11,1... | collective-permute-start | bytes 1572872 | tf_op jit(solution)/shard_map/ppermute | solution.py:190
  412.2 1.0 copy-start.5
  413.2 14.0 %copy-start.6 = (bf16[10,27,4096]{2,1,0:T(8,128)(2,1)S(1)}, bf16[10,27,4096]{2,1,0:T(8,128)(2,1)}, u32[]{:S(2)}) copy-start(bf16[10,27,4096]{2,1,0:T(8,128)(2,1)} %reshape.68) | copy-start | bytes 6635524
  413.2 14.0 %copy-start.7 = (bf16[2,27,4096]{2,1,0:T(8,128)(2,1)S(1)}, bf16[2,27,4096]{2,1,0:T(8,128)(2,1)}, u32[]{:S(2)}) copy-start(bf16[2,27,4096]{2,1,0:T(8,128)(2,1)} %all_gather.11) | copy-start | bytes 1327108
Sparse Core Ops, SparseCore 0:
  95.9 25.1 reduce-scatter.7
  123.4 49.9 reduce-scatter.3
  175.8 52.3 all-reduce.2
  231.0 23.7 reduce-scatter.5
  258.0 54.2 all-reduce.4
  315.0 61.0 all-gather.2

commit v2 on v1

--- a/solution.py
+++ b/solution.py
@@ -163,6 +163,170 @@
     lax.fori_loop(0, thick * per_plane, second, 0)
 
 
+def flipped(index, bit):
+    return index + (1 << bit) * (1 - 2 * lax.rem(index // (1 << bit), 2))
+
+
+def crossed(left, right, bits):
+    total = 0
+    for bit in range(bits):
+        one = lax.rem(left // (1 << bit), 2)
+        two = lax.rem(right // (1 << bit), 2)
+        total = total + (1 << bit) * (one + two - 2 * one * two)
+    return total
+
+
+def subset(bits):
+    sums = [0]
+    for bit in bits:
+        sums = sums + [one + bit for one in sums]
+    return sums
+
+
+def owner_kernel(
+    replicas, slabs, scale,
+    tensor_of, used, assignment, grads, first, second, master,
+    params, out_first, out_second, out_master,
+    work, landed, held, send_one, recv_one, send_two, recv_two,
+):
+    slots, taps, share = first.shape
+    me, lane = lax.axis_index("dp"), lax.axis_index("space")
+    dp_bits, space_bits = replicas.bit_length() - 1, slabs.bit_length() - 1
+    core = lax.rem(me, 2)
+    turn = [(k, (k + 1) % space_bits) for k in range(space_bits)]
+    weight = [(1 - core) * (1 << one) + core * (1 << two) for one, two in turn]
+    by_core = (flipped(me, 0), lane)
+    by_space = [
+        (me, (1 - core) * flipped(lane, one) + core * flipped(lane, two)) for one, two in turn
+    ]
+    by_dp = [(flipped(me, bit), lane) for bit in range(1, dp_bits)]
+
+    barrier = pltpu.get_barrier_semaphore()
+    for partner in [by_core] + by_space + by_dp:
+        pl.semaphore_signal(
+            barrier, inc=1, device_id=partner, device_id_type=pl.DeviceIdType.MESH
+        )
+    pl.semaphore_wait(barrier, dp_bits + space_bits)
+
+    def build(odd):
+        def one(n, _):
+            apart = 2 * (n // slabs) + odd
+            aside = lax.rem(n, slabs)
+            owner = crossed(me, apart, dp_bits)
+            column = crossed(lane, aside, space_bits)
+            columns = pl.ds(pl.multiple_of(column * share, share), share)
+            for slot in range(slots):
+                number = owner * slots + slot
+                value = grads[tensor_of[number], :, columns].astype(jnp.float32)
+                work[apart * slabs + aside, slot] = (value * used[number]).astype(jnp.bfloat16)
+            return 0
+
+        lax.fori_loop(0, replicas * slabs // 2, one, 0)
+
+    steps = [
+        (
+            by_core,
+            [
+                ((rd + 1) * slabs + rs, rd * slabs + rs)
+                for rd in range(0, replicas, 2)
+                for rs in range(slabs)
+            ],
+        )
+    ]
+    for k in range(space_bits):
+        later = subset(weight[k + 1 :][::-1])[::-1]
+        pairs = [
+            (rd * slabs + rs + weight[k], rd * slabs + rs)
+            for rs in later
+            for rd in range(0, replicas, 2)
+        ]
+        steps.append((by_space[k], pairs))
+    for bit in range(1, dp_bits):
+        later = subset([1 << j for j in range(bit + 1, dp_bits)][::-1])[::-1]
+        pairs = [((rd + (1 << bit)) * slabs, rd * slabs) for rd in later]
+        steps.append((by_dp[bit - 1], pairs))
+
+    count = 0
+    pending, sent = [], []
+    for number, (partner, pairs) in enumerate(steps):
+        if number == 0:
+            build(1)
+        copies = []
+        for source, target in pairs:
+            copy = pltpu.make_async_remote_copy(
+                src_ref=work.at[source],
+                dst_ref=landed.at[count],
+                send_sem=send_one.at[count],
+                recv_sem=recv_one.at[count],
+                device_id=partner,
+                device_id_type=pl.DeviceIdType.MESH,
+            )
+            copy.start()
+            copies.append((copy, target, count))
+            count += 1
+        if number == 0:
+            build(0)
+        for copy, target, at in copies:
+            copy.wait_recv()
+            total = work[target].astype(jnp.float32) + landed[at].astype(jnp.float32)
+            work[target] = total.astype(jnp.bfloat16)
+            sent.append(copy)
+    for copy in sent:
+        copy.wait_send()
+
+    owned = work[0].astype(jnp.float32) * scale
+    new_first = 0.9 * first[...] + 0.1 * owned
+    new_second = 0.999 * second[...] + 0.001 * owned * owned
+    update = new_first / bias_one / (jnp.sqrt(new_second / bias_two) + epsilon)
+    new_master = master[...] - learn_rate * (update + decay_rate * master[...])
+    out_first[...] = new_first
+    out_second[...] = new_second
+    out_master[...] = new_master
+    held[0] = new_master.astype(jnp.bfloat16)
+
+    count = 0
+    have = [0]
+    sent = []
+    moves = [(by_dp[bit - 1], (1 << bit) * slabs) for bit in range(dp_bits - 1, 0, -1)]
+    moves += [(by_space[k], weight[k]) for k in range(space_bits - 1, -1, -1)]
+    moves.append((by_core, slabs))
+    for number, (partner, gap) in enumerate(moves):
+        if number == len(moves) - 1:
+            have = [rd * slabs + rs for rd in range(0, replicas, 2) for rs in range(slabs)]
+        copies = []
+        for source in have:
+            copy = pltpu.make_async_remote_copy(
+                src_ref=held.at[source],
+                dst_ref=held.at[source + gap],
+                send_sem=send_two.at[count],
+                recv_sem=recv_two.at[count],
+                device_id=partner,
+                device_id_type=pl.DeviceIdType.MESH,
+            )
+            copy.start()
+            copies.append(copy)
+            count += 1
+        for copy in copies:
+            copy.wait_recv()
+        sent += copies
+        have = have + [one + gap for one in have]
+    for copy in sent:
+        copy.wait_send()
+
+    for column in range(slabs):
+        aside = crossed(lane, column, space_bits)
+
+        def place(tensor, _, column=column, aside=aside):
+            slot = assignment[tensor]
+            apart = crossed(me, slot // slots, dp_bits)
+            params[tensor, :, column * share : (column + 1) * share] = held[
+                apart * slabs + aside, lax.rem(slot, slots)
+            ]
+            return 0
+
+        lax.fori_loop(0, params.shape[0], place, 0)
+
+
 def whole(count):
     return [pl.BlockSpec(memory_space=pltpu.VMEM)] * count
 
@@ -189,14 +353,6 @@
     low = lax.ppermute(field, "space", forward)
     high = lax.ppermute(field, "space", backward)
     return low, field, high
-
-
-def adamw(moment_first, moment_second, master_weights, grads):
-    new_first = 0.9 * moment_first + 0.1 * grads
-    new_second = 0.999 * moment_second + 0.001 * grads * grads
-    update = new_first / bias_one / (jnp.sqrt(new_second / bias_two) + epsilon)
-    new_master = master_weights - learn_rate * (update + decay_rate * master_weights)
-    return new_first, new_second, new_master
 
 
 def per_device(
@@ -219,16 +375,6 @@
     cells = rows * lanes
     scale = 1.0 / math.sqrt(replicas * thick * slabs * cells)
     params = pltpu.CompilerParams(vmem_limit_bytes=48 * 1024 * 1024)
-
-    match = assignment[None, :] == jnp.arange(every_slot, dtype=jnp.int32)[:, None]
-    used = jnp.any(match, axis=1)
-    tensor_of = jnp.argmax(match, axis=1).astype(jnp.int32)
-    by_slot = jnp.where(
-        used[:, None, None], jnp.take(other_grads[0, 0], tensor_of, axis=0), 0
-    ).astype(jnp.bfloat16)
-    owned = lax.psum_scatter(by_slot, "dp", scatter_dimension=0, tiled=True)
-    owned = lax.psum_scatter(owned, "space", scatter_dimension=2, tiled=True)
-    owned = owned.astype(jnp.float32)
 
     dec = neighbours(decoder_input[0].transpose(1, 2, 0, 3))
     cot = neighbours(cotangent[0].transpose(1, 2, 0, 3))
@@ -262,32 +408,39 @@
     input_grad = input_grad.transpose(2, 0, 1, 3)[None]
 
     pair = jnp.stack([unstacked(grad_a, channels), unstacked(grad_b, channels)])
-    pair = lax.psum_scatter(pair.astype(bf), "space", scatter_dimension=2, tiled=True)
-    pair = lax.psum(pair, "dp").astype(jnp.float32)
-
-    mine = lax.axis_index("dp") * slots + jnp.arange(slots, dtype=jnp.int32)
-    early = adamw(moment_first, moment_second, master_weights, owned * scale)[2]
-    gathered = lax.all_gather(early.astype(bf), ("dp", "space"), axis=0)
-    gathered = gathered.reshape(replicas, slabs, slots, taps, share)
-    picked = gathered[assignment // slots, :, lax.rem(assignment, slots)]
-
-    is_a = (mine == assignment[0])[:, None, None]
-    is_b = (mine == assignment[1])[:, None, None]
-    owned = owned + jnp.where(is_a, pair[0], 0.0) + jnp.where(is_b, pair[1], 0.0)
-    new_first, new_second, new_master = adamw(
-        moment_first, moment_second, master_weights, owned * scale
-    )
-    rounded = new_master.astype(bf)
-    late = jnp.stack(
-        [
-            jnp.sum(jnp.where(is_a, rounded, 0), axis=0),
-            jnp.sum(jnp.where(is_b, rounded, 0), axis=0),
+    match = assignment[None, :] == jnp.arange(every_slot, dtype=jnp.int32)[:, None]
+    used = jnp.any(match, axis=1).astype(jnp.float32)
+    tensor_of = jnp.argmax(match, axis=1).astype(jnp.int32)
+    mixed = (other_grads[0, 0, :2].astype(jnp.float32) + pair).astype(bf)
+    grads = jnp.concatenate([mixed, other_grads[0, 0, 2:]], axis=0)
+    chunks = replicas * slabs
+    state = jax.ShapeDtypeStruct(moment_first.shape, jnp.float32)
+    scalars = [pl.BlockSpec(memory_space=pltpu.SMEM)] * 3
+    new_params, new_first, new_second, new_master = pl.pallas_call(
+        functools.partial(owner_kernel, replicas, slabs, scale),
+        out_shape=(
+            jax.ShapeDtypeStruct((tensors, taps, slabs * share), bf),
+            state,
+            state,
+            state,
+        ),
+        in_specs=scalars + whole(4),
+        out_specs=tuple(whole(4)),
+        scratch_shapes=[
+            pltpu.VMEM((chunks, slots, taps, share), bf),
+            pltpu.VMEM((chunks - 1, slots, taps, share), bf),
+            pltpu.VMEM((chunks, slots, taps, share), bf),
         ]
-    ).astype(bf)
-    late = lax.psum(late, "dp")
-    late = lax.all_gather(late, "space", axis=2, tiled=True)
-    rest = picked[2:].transpose(0, 2, 1, 3).reshape(tensors - 2, taps, slabs * share)
-    new_params = jnp.concatenate([late, rest], axis=0)
+        + [pltpu.SemaphoreType.DMA((chunks - 1,))] * 4,
+        compiler_params=pltpu.CompilerParams(
+            vmem_limit_bytes=56 * 1024 * 1024, collective_id=0, has_side_effects=True
+        ),
+        cost_estimate=pl.CostEstimate(
+            flops=2**24, bytes_accessed=16 * 2**20, transcendentals=0
+        ),
+        name="owners",
+    )(tensor_of, used, assignment, grads, moment_first, moment_second, master_weights)
+    rest = new_params[2:4]
 
     enc = neighbours(encoder_input[0].transpose(1, 2, 0, 3))
     w_c = stacked_weights(rest[0], channels)

time: 438 us -> 206 us (0.47)
  the two profiles are of different devices: /device:TPU:0 before, /device:TPU:9 now
where the time goes in v2:
time: 206 us; the launch traced here: 205 us
  Pallas kernels  129 us (63%)
  local copies, waits for them, and re-layouts  57.6 us (28%)
  starting transfers between devices  7.25 us (4%)
  other arithmetic  6.16 us (3%)
  waiting for transfers between devices  4.89 us (2%)
    pallas_call x1, Pallas kernels, per_device(): pl.pallas_call(functools.partial(owner_kernel, replicas, slabs, scale), o...  96.5 us
    unnamed x46, local copies, waits for them, and re-layouts  22.9 us
    pallas_call x1, Pallas kernels, per_device(): pl.pallas_call(functools.partial(decoder_kernel, rows), out_shape=(field,...  19.5 us
    pallas_call x1, Pallas kernels, per_device(): pl.pallas_call(functools.partial(encoder_kernel, rows), out_shape=field,...  12.6 us
    transpose x4, local copies, waits for them, and re-layouts, turned_weights(): return taps.transpose(0, 2, 4, 1, 3).reshape(3, 3 * channels, 3 * channels)  6.81 us
    ppermute x3, starting transfers between devices, neighbours(): high = lax.ppermute(field, 'space', backward)  5.51 us
    ppermute x3, waiting for transfers between devices, neighbours(): high = lax.ppermute(field, 'space', backward)  4.88 us
    reshape x2, local copies, waits for them, and re-layouts, turned_weights(): return taps.transpose(0, 2, 4, 1, 3).reshape(3, 3 * channels, 3 * channels)  4.33 us
  transfers between devices with their start and end apart: 6, of which 1 were waited for; matrix products, arithmetic and copies ran while one was open for 23% of the time, Pallas kernels for 57%

profile of v2, /device:TPU:9, one launch (start us, length us, event | category | flops | bytes accessed | tf_op | source)
XLA Modules:
  0.0 205.3 jit_solution(11805579446761407730)
XLA Ops:
  0.6 1.3 copy.78
  1.9 1.3 collective-permute-start
  3.2 1.2 collective-permute-start.1
  4.4 1.2 copy.77
  6.0 2.1 collective-permute-start.3
  8.0 1.2 copy.76
  9.4 2.5 %slice_reduce_fusion = (bf16[27,4096]{1,0:T(8,128)(2,1)S(1)}, bf16[27,4096]{1,0:T(8,128)(2,1)}) fusion(bf16[2,27,4096]{2,0,1:T(2,128)(2,1)S(1)} %copy-done.11), kind=kLoop, calls=%fused_computation.11 | loop fusion | bytes 884736 | tf_op jit(solution)/shard_map/slice | solution.py:383
  11.9 2.2 %reshape_squeeze.13 = bf16[3,3,3,64,64]{4,3,2,1,0:T(8,128)(2,1)} reshape(bf16[27,4096]{1,0:T(8,128)(2,1)} %get-tuple-element.41) | data formatting | bytes 442368 | tf_op jit(solution)/shard_map/reshape;squeeze | solution.py:335
  14.1 3.6 %slice_bitcast_fusion = bf16[10,27,4096]{2,1,0:T(8,128)(2,1)} fusion(bf16[1,1,12,27,4096]{4,3,2,1,0:T(8,128)(2,1)} %param.13), kind=kLoop, calls=%fused_computation.1 | loop fusion | bytes 4423680 | tf_op jit(solution)/shard_map/squeeze | solution.py:415
  17.7 0.8 reverse_bitcast_fusion
  18.5 2.1 %copy.55 = bf16[3,3,64,3,64]{4,3,2,1,0:T(4,128)(2,1)} copy(bf16[3,3,64,3,64]{2,4,1,3,0:T(8,128)(2,1)} %reverse_bitcast_fusion) | data formatting | bytes 442368 | tf_op jit(solution)/shard_map/transpose | solution.py:341
  20.6 2.2 %reshape.38.w_at = bf16[3,192,192]{2,1,0:T(8,128)(2,1)} reshape(bf16[3,3,64,3,64]{4,3,2,1,0:T(4,128)(2,1)} %copy.55) | data formatting | bytes 442368 | tf_op jit(solution)/shard_map/reshape | solution.py:341
  22.8 2.2 %copy.53 = bf16[3,3,64,3,64]{4,3,2,1,0:T(4,128)(2,1)} copy(bf16[3,3,64,3,64]{4,2,1,3,0:T(8,128)(2,1)} %bitcast.56) | data formatting | bytes 442368 | tf_op jit(solution)/shard_map/transpose | solution.py:336
  25.0 2.2 %reshape.36.w_a = bf16[3,192,192]{2,1,0:T(8,128)(2,1)} reshape(bf16[3,3,64,3,64]{4,3,2,1,0:T(4,128)(2,1)} %copy.53) | data formatting | bytes 442368 | tf_op jit(solution)/shard_map/reshape | solution.py:336
  27.2 1.2 reshape_squeeze.14
  28.4 1.8 reverse_bitcast_fusion.1
  30.2 2.1 %copy.54 = bf16[3,3,64,3,64]{4,3,2,1,0:T(4,128)(2,1)} copy(bf16[3,3,64,3,64]{2,4,1,3,0:T(8,128)(2,1)} %reverse_bitcast_fusion.1) | data formatting | bytes 442368 | tf_op jit(solution)/shard_map/transpose | solution.py:341
  32.3 2.2 %reshape.37.w_bt = bf16[3,192,192]{2,1,0:T(8,128)(2,1)} reshape(bf16[3,3,64,3,64]{4,3,2,1,0:T(4,128)(2,1)} %copy.54) | data formatting | bytes 442368 | tf_op jit(solution)/shard_map/reshape | solution.py:341
  34.5 1.7 copy.59.first
  36.2 0.8 copy.60.second
  37.0 1.7 copy.61.master
  40.0 0.8 copy-done.3
  40.8 2.3 %collective-permute-start.5 = (bf16[2,16,64,128]{3,2,1,0:T(8,128)(2,1)S(1)}, bf16[2,16,64,128]{3,2,1,0:T(8,128)(2,1)}, u32[]{:S(2)}, u32[]{:S(2)}) collective-permute-start(bf16[2,16,64,128]{3,2,1,0:T(8,128)(2,1)S(1)} %bitcast.44), channel_id=1, source_target_pairs={{1,0},{2,1},{3,2},{0,3},{5,4},{6,5},{7,6},{4,7},{9,8},{10,9},{11,1... | collective-permute-start | bytes 1572872 | tf_op jit(solution)/shard_map/ppermute | solution.py:354
  43.1 0.8 copy-done.5
  43.9 0.8 copy-done.7
  44.7 4.9 %collective-permute-done.3.cot_high = bf16[2,16,64,128]{3,2,1,0:T(8,128)(2,1)} collective-permute-done((bf16[2,16,64,128]{3,2,1,0:T(8,128)(2,1)S(1)}, bf16[2,16,64,128]{3,2,1,0:T(8,128)(2,1)}, u32[]{:S(2)}, u32[]{:S(2)}) %collective-permute-start.3) | collective-permute-done | bytes 524320 | tf_op jit(solution)/shard_map/ppermute | solution.py:354
  49.6 1.0 copy-done
  50.5 1.0 copy-done.1
  51.5 1.0 copy-done.2
  52.4 1.0 copy-done.4
  53.5 1.0 copy-done.6
  54.5 1.0 copy-done.8
  55.6 19.5 %decoder.1 = (bf16[2,16,64,128]{3,2,1,0:T(8,128)(2,1)S(1)}, f32[3,192,192]{2,1,0:T(8,128)S(1)}, f32[3,192,192]{2,1,0:T(8,128)S(1)}) custom-call(bf16[2,16,64,128]{3,2,1,0:T(8,128)(2,1)S(1)} %copy-done.4, bf16[2,16,64,128]{3,2,1,0:T(8,128)(2,1)S(1)} %bitcast.49, bf16[2,16,64,128]{3,2,1,0:T(8,128)(2,1)S(1)} %copy-done.6, ...), custom_call_target="tpu_custom_call" | custom-call | flops 13589544960 | bytes 8388608 | tf_op jit(solution)/shard_map/decoder/pallas_call | solution.py:389
  75.1 1.4 reshape.39
  76.5 1.4 copy.57
  78.2 1.4 reshape.40
  79.6 1.4 copy.58
  81.3 1.1 fusion
  82.4 3.7 %pad_maximum_fusion.grads = bf16[12,27,4096]{2,1,0:T(8,128)(2,1)} fusion(bf16[10,27,4096]{2,1,0:T(8,128)(2,1)} %slice_bitcast_fusion, bf16[2,27,4096]{2,1,0:T(8,128)(2,1)S(1)} %fusion), kind=kLoop, calls=%fused_computation | loop fusion | flops 1327104 | bytes 5308416 | tf_op jit(solution)/shard_map/concatenate | solution.py:415
  86.2 96.5 %owners.1 = (bf16[12,27,4096]{2,1,0:T(8,128)(2,1)}, f32[2,27,1024]{2,1,0:T(8,128)}, f32[2,27,1024]{2,1,0:T(8,128)}, f32[2,27,1024]{2,1,0:T(8,128)}) custom-call(s32[16]{0:T(128)} %get-tuple-element.15.tensor_of, f32[16]{0:T(128)} %convert_element_type.12.used, s32[12]{0:T(128)} %assignment.1, bf16[12,27,4096]{2,1,0:T(8,128)(2,1)} %pad_maximum_fusion.grads, ...), custom_call_target="tpu_custom_call" | custom-call | flops 16777216 | bytes 16777216 | tf_op jit(solution)/shard_map/owners/pallas_call | solution.py:419
  182.7 1.1 fusion.2
  186.2 12.6 %encoder.1 = bf16[2,16,64,128]{3,2,1,0:T(8,128)(2,1)S(1)} custom-call(bf16[2,16,64,128]{3,2,1,0:T(8,128)(2,1)} %collective-permute-done.4.low, bf16[2,16,64,128]{3,2,1,0:T(8,128)(2,1)S(1)} %bitcast.45, bf16[2,16,64,128]{3,2,1,0:T(8,128)(2,1)} %collective-permute-done.5.high, bf16[3,192,192]{2,1,0:T(8,128)(2,1)S(1)} %reshape.41.w_c, ...), custom_call_target="tpu_custom_call" | custom-call | flops 5435817984 | bytes 4194304 | tf_op jit(solution)/shard_map/encoder/pallas_call | solution.py:448
  198.8 1.1 copy.65
  200.0 0.9 copy.66
  200.8 0.9 copy.67
  201.7 0.9 copy.68
  202.5 1.1 copy.64
  203.7 1.7 copy.80
  (43 shorter events, 4.8 us)
Async XLA Ops:
  0.6 8.8 %copy-start.11 = (bf16[2,27,4096]{2,0,1:T(2,128)(2,1)S(1)}, bf16[2,27,4096]{2,0,1:T(2,128)(2,1)}, u32[]{:S(2)}) copy-start(bf16[2,27,4096]{2,0,1:T(2,128)(2,1)} %param.12) | copy-start | bytes 1327108
  1.9 38.0 %collective-permute-start = (bf16[2,16,64,128]{3,2,1,0:T(8,128)(2,1)S(1)}, bf16[2,16,64,128]{3,2,1,0:T(8,128)(2,1)S(1)}, u32[]{:S(2)}, u32[]{:S(2)}) collective-permute-start(bf16[2,16,64,128]{3,2,1,0:T(8,128)(2,1)S(1)} %bitcast.47), channel_id=1, source_target_pairs={{0,1},{1,2},{2,3},{3,0},{4,5},{5,6},{6,7},{7,4},{8,9},{9,10},{10,1... | collective-permute-start | bytes 1572872 | tf_op jit(solution)/shard_map/ppermute | solution.py:353
  3.2 39.9 %collective-permute-start.1 = (bf16[2,16,64,128]{3,2,1,0:T(8,128)(2,1)S(1)}, bf16[2,16,64,128]{3,2,1,0:T(8,128)(2,1)S(1)}, u32[]{:S(2)}, u32[]{:S(2)}) collective-permute-start(bf16[2,16,64,128]{3,2,1,0:T(8,128)(2,1)S(1)} %bitcast.48), channel_id=1, source_target_pairs={{1,0},{2,1},{3,2},{0,3},{5,4},{6,5},{7,6},{4,7},{9,8},{10,9},{11,1... | collective-permute-start | bytes 1572872 | tf_op jit(solution)/shard_map/ppermute | solution.py:354
  5.6 38.3 %collective-permute-start.2 = (bf16[2,16,64,128]{3,2,1,0:T(8,128)(2,1)S(1)}, bf16[2,16,64,128]{3,2,1,0:T(8,128)(2,1)S(1)}, u32[]{:S(2)}, u32[]{:S(2)}) collective-permute-start(bf16[2,16,64,128]{3,2,1,0:T(8,128)(2,1)S(1)} %bitcast.50), channel_id=1, source_target_pairs={{0,1},{1,2},{2,3},{3,0},{4,5},{5,6},{6,7},{7,4},{8,9},{9,10},{10,1... | collective-permute-start | bytes 1572872 | tf_op jit(solution)/shard_map/ppermute | solution.py:353
  6.0 43.6 %collective-permute-start.3 = (bf16[2,16,64,128]{3,2,1,0:T(8,128)(2,1)S(1)}, bf16[2,16,64,128]{3,2,1,0:T(8,128)(2,1)}, u32[]{:S(2)}, u32[]{:S(2)}) collective-permute-start(bf16[2,16,64,128]{3,2,1,0:T(8,128)(2,1)S(1)} %bitcast.51), channel_id=1, source_target_pairs={{1,0},{2,1},{3,2},{0,3},{5,4},{6,5},{7,6},{4,7},{9,8},{10,9},{11,1... | collective-permute-start | bytes 1572872 | tf_op jit(solution)/shard_map/ppermute | solution.py:354
  9.3 176.9 %collective-permute-start.4 = (bf16[2,16,64,128]{3,2,1,0:T(8,128)(2,1)S(1)}, bf16[2,16,64,128]{3,2,1,0:T(8,128)(2,1)}, u32[]{:S(2)}, u32[]{:S(2)}) collective-permute-start(bf16[2,16,64,128]{3,2,1,0:T(8,128)(2,1)S(1)} %bitcast.43), channel_id=1, source_target_pairs={{0,1},{1,2},{2,3},{3,0},{4,5},{5,6},{6,7},{7,4},{8,9},{9,10},{10,1... | collective-permute-start | bytes 1572872 | tf_op jit(solution)/shard_map/ppermute | solution.py:353
  14.1 3.6 %copy-start.10 = (bf16[3,3,3,64,64]{4,3,2,1,0:T(8,128)(2,1)S(1)}, bf16[3,3,3,64,64]{4,3,2,1,0:T(8,128)(2,1)}, u32[]{:S(2)}) copy-start(bf16[3,3,3,64,64]{4,3,2,1,0:T(8,128)(2,1)} %reshape_squeeze.13) | copy-start | bytes 663556
  25.0 13.7 %copy-start.16 = (s32[12]{0:T(128)S(1)}, s32[12]{0:T(128)}, u32[]{:S(2)}) copy-start(s32[12]{0:T(128)} %assignment.1) | copy-start | bytes 148
  28.4 7.8 %copy-start.15 = (f32[2,27,1024]{2,0,1:T(2,128)S(1)}, f32[2,27,1024]{2,0,1:T(2,128)}, u32[]{:S(2)}) copy-start(f32[2,27,1024]{2,0,1:T(2,128)} %param.16) | copy-start | bytes 663556
  40.0 0.8 copy-start.3
  40.8 145.4 %collective-permute-start.5 = (bf16[2,16,64,128]{3,2,1,0:T(8,128)(2,1)S(1)}, bf16[2,16,64,128]{3,2,1,0:T(8,128)(2,1)}, u32[]{:S(2)}, u32[]{:S(2)}) collective-permute-start(bf16[2,16,64,128]{3,2,1,0:T(8,128)(2,1)S(1)} %bitcast.44), channel_id=1, source_target_pairs={{1,0},{2,1},{3,2},{0,3},{5,4},{6,5},{7,6},{4,7},{9,8},{10,9},{11,1... | collective-permute-start | bytes 1572872 | tf_op jit(solution)/shard_map/ppermute | solution.py:354
  43.1 0.8 copy-start.5
  43.9 0.8 copy-start.7
  49.6 1.0 copy-start
  50.5 1.0 copy-start.1
  51.5 1.0 copy-start.2
  52.4 1.0 copy-start.4
  53.5 1.0 copy-start.6
  54.5 1.0 copy-start.8
  186.1 13.8 %copy-start.14 = (f32[2,27,1024]{2,1,0:T(8,128)S(1)}, f32[2,27,1024]{2,1,0:T(8,128)}, u32[]{:S(2)}) copy-start(f32[2,27,1024]{2,1,0:T(8,128)} %get-tuple-element.37) | copy-start | bytes 663556
  186.1 14.7 %copy-start.13 = (f32[2,27,1024]{2,1,0:T(8,128)S(1)}, f32[2,27,1024]{2,1,0:T(8,128)}, u32[]{:S(2)}) copy-start(f32[2,27,1024]{2,1,0:T(8,128)} %get-tuple-element.38) | copy-start | bytes 663556
  186.1 15.5 %copy-start.12 = (f32[2,27,1024]{2,1,0:T(8,128)S(1)}, f32[2,27,1024]{2,1,0:T(8,128)}, u32[]{:S(2)}) copy-start(f32[2,27,1024]{2,1,0:T(8,128)} %get-tuple-element.39) | copy-start | bytes 663556
  198.8 4.9 %copy-start.9 = (bf16[12,27,4096]{2,1,0:T(8,128)(2,1)S(1)}, bf16[12,27,4096]{2,1,0:T(8,128)(2,1)}, u32[]{:S(2)}) copy-start(bf16[12,27,4096]{2,1,0:T(8,128)(2,1)} %get-tuple-element.52) | copy-start | bytes 7962628

commit v3 on v2

--- a/solution.py
+++ b/solution.py
@@ -176,13 +176,6 @@
     return total
 
 
-def subset(bits):
-    sums = [0]
-    for bit in bits:
-        sums = sums + [one + bit for one in sums]
-    return sums
-
-
 def owner_kernel(
     replicas, slabs, scale,
     tensor_of, used, assignment, grads, first, second, master,
@@ -223,54 +216,78 @@
 
         lax.fori_loop(0, replicas * slabs // 2, one, 0)
 
-    steps = [
-        (
-            by_core,
-            [
-                ((rd + 1) * slabs + rs, rd * slabs + rs)
-                for rd in range(0, replicas, 2)
-                for rs in range(slabs)
-            ],
+    order = [by_core] + by_space + by_dp
+
+    def place_of(chunk):
+        core_bit, turns, rest = chunk[0], chunk[1 : 1 + space_bits], chunk[1 + space_bits :]
+        apart = core_bit + sum(bit << (k + 1) for k, bit in enumerate(rest))
+        index = apart * slabs
+        for bit, amount in zip(turns, weight):
+            index = index + amount * bit
+        return index
+
+    depth = dp_bits + space_bits
+    half = replicas * slabs // 2
+
+    def core_number(chunk):
+        rest = sum(bit << k for k, bit in enumerate(chunk[1 + space_bits :]))
+        index = rest * slabs
+        for bit, amount in zip(chunk[1 : 1 + space_bits], weight):
+            index = index + amount * bit
+        return index
+
+    def tails(length):
+        out = [()]
+        for _ in range(length):
+            out = [(bit,) + tail for bit in (1, 0) for tail in out]
+        return out
+
+    numbers, count = {}, half
+    for step in range(1, depth):
+        for tail in tails(depth - 1 - step):
+            numbers[(0,) * step + (1,) + tail] = count
+            count += 1
+
+    def number_of(chunk):
+        return core_number(chunk) if chunk[0] else numbers[chunk]
+
+    sent = []
+
+    def send(chunk, step, source, target, send_sem, recv_sem, number):
+        copy = pltpu.make_async_remote_copy(
+            src_ref=source,
+            dst_ref=target,
+            send_sem=send_sem.at[number],
+            recv_sem=recv_sem.at[number],
+            device_id=order[step],
+            device_id_type=pl.DeviceIdType.MESH,
         )
-    ]
-    for k in range(space_bits):
-        later = subset(weight[k + 1 :][::-1])[::-1]
-        pairs = [
-            (rd * slabs + rs + weight[k], rd * slabs + rs)
-            for rs in later
-            for rd in range(0, replicas, 2)
-        ]
-        steps.append((by_space[k], pairs))
-    for bit in range(1, dp_bits):
-        later = subset([1 << j for j in range(bit + 1, dp_bits)][::-1])[::-1]
-        pairs = [((rd + (1 << bit)) * slabs, rd * slabs) for rd in later]
-        steps.append((by_dp[bit - 1], pairs))
-
-    count = 0
-    pending, sent = [], []
-    for number, (partner, pairs) in enumerate(steps):
-        if number == 0:
-            build(1)
-        copies = []
-        for source, target in pairs:
-            copy = pltpu.make_async_remote_copy(
-                src_ref=work.at[source],
-                dst_ref=landed.at[count],
-                send_sem=send_one.at[count],
-                recv_sem=recv_one.at[count],
-                device_id=partner,
-                device_id_type=pl.DeviceIdType.MESH,
-            )
-            copy.start()
-            copies.append((copy, target, count))
-            count += 1
-        if number == 0:
-            build(0)
-        for copy, target, at in copies:
-            copy.wait_recv()
-            total = work[target].astype(jnp.float32) + landed[at].astype(jnp.float32)
-            work[target] = total.astype(jnp.bfloat16)
-            sent.append(copy)
+        copy.start()
+        sent.append(copy)
+        return copy
+
+    def reduce_send(chunk, step):
+        number = number_of(chunk)
+        return send(
+            chunk, step, work.at[place_of(chunk)], landed.at[number], send_one, recv_one, number
+        )
+
+    build(1)
+    flying = {}
+    for tail in tails(depth - 1):
+        chunk = (1,) + tail
+        flying[chunk] = reduce_send(chunk, 0)
+    build(0)
+    for step in range(depth):
+        for tail in tails(depth - 1 - step):
+            came = (0,) * step + (1,) + tail
+            target = (0,) * (step + 1) + tail
+            flying[came].wait_recv()
+            at, number = place_of(target), number_of(came)
+            total = work[at].astype(jnp.float32) + landed[number].astype(jnp.float32)
+            work[at] = total.astype(jnp.bfloat16)
+            if tail and tail[0]:
+                flying[target] = reduce_send(target, step + 1)
     for copy in sent:
         copy.wait_send()
 
@@ -284,32 +301,26 @@
     out_master[...] = new_master
     held[0] = new_master.astype(jnp.bfloat16)
 
-    count = 0
-    have = [0]
-    sent = []
-    moves = [(by_dp[bit - 1], (1 << bit) * slabs) for bit in range(dp_bits - 1, 0, -1)]
-    moves += [(by_space[k], weight[k]) for k in range(space_bits - 1, -1, -1)]
-    moves.append((by_core, slabs))
-    for number, (partner, gap) in enumerate(moves):
-        if number == len(moves) - 1:
-            have = [rd * slabs + rs for rd in range(0, replicas, 2) for rs in range(slabs)]
-        copies = []
-        for source in have:
-            copy = pltpu.make_async_remote_copy(
-                src_ref=held.at[source],
-                dst_ref=held.at[source + gap],
-                send_sem=send_two.at[count],
-                recv_sem=recv_two.at[count],
-                device_id=partner,
-                device_id_type=pl.DeviceIdType.MESH,
-            )
-            copy.start()
-            copies.append(copy)
-            count += 1
-        for copy in copies:
+    sent.clear()
+
+    def spread(chunk, step):
+        came = chunk[:step] + (1,) + chunk[step + 1 :]
+        number = number_of(came)
+        return send(
+            came, step, held.at[place_of(chunk)], held.at[place_of(came)], send_two, recv_two, number
+        )
+
+    have, core_copies = [(0,) * depth], []
+    core_copies.append(spread(have[0], 0))
+    for step in range(depth - 1, 0, -1):
+        copies = [spread(chunk, step) for chunk in have]
+        came = [chunk[:step] + (1,) + chunk[step + 1 :] for chunk in have]
+        for copy, chunk in zip(copies, came):
             copy.wait_recv()
-        sent += copies
-        have = have + [one + gap for one in have]
+            core_copies.append(spread(chunk, 0))
+        have = have + came
+    for copy in core_copies:
+        copy.wait_recv()
     for copy in sent:
         copy.wait_send()
 

time: 206 us -> 196 us (0.951)
  the two profiles are of different devices: /device:TPU:9 before, /device:TPU:0 now
where the time goes in v3:
time: 196 us; the launch traced here: 193 us
  Pallas kernels  113 us (58%)
  local copies, waits for them, and re-layouts  57.6 us (29%)
  starting transfers between devices  9.97 us (5%)
  other arithmetic  6.16 us (3%)
  waiting for transfers between devices  5.64 us (3%)
    pallas_call x1, Pallas kernels, per_device(): pl.pallas_call(functools.partial(owner_kernel, replicas, slabs, scale), o...  80.7 us
    unnamed x46, local copies, waits for them, and re-layouts  22.9 us
    pallas_call x1, Pallas kernels, per_device(): pl.pallas_call(functools.partial(decoder_kernel, rows), out_shape=(field,...  19.5 us
    pallas_call x1, Pallas kernels, per_device(): pl.pallas_call(functools.partial(encoder_kernel, rows), out_shape=field,...  12.7 us
    transpose x4, local copies, waits for them, and re-layouts, turned_weights(): return taps.transpose(0, 2, 4, 1, 3).reshape(3, 3 * channels, 3 * channels)  6.81 us
    ppermute x3, waiting for transfers between devices, neighbours(): high = lax.ppermute(field, 'space', backward)  5.63 us
    ppermute x3, starting transfers between devices, neighbours(): high = lax.ppermute(field, 'space', backward)  5.39 us
    ppermute x3, starting transfers between devices, neighbours(): low = lax.ppermute(field, 'space', forward)  4.57 us
  transfers between devices with their start and end apart: 6, of which 1 were waited for; matrix products, arithmetic and copies ran while one was open for 25% of the time, Pallas kernels for 52%

profile of v3, /device:TPU:0, one launch (start us, length us, event | category | flops | bytes accessed | tf_op | source)
XLA Modules:
  0.0 193.1 jit_solution(9559356810277194829)
XLA Ops:
  0.6 1.3 copy.78
  1.9 3.0 %collective-permute-start = (bf16[2,16,64,128]{3,2,1,0:T(8,128)(2,1)S(1)}, bf16[2,16,64,128]{3,2,1,0:T(8,128)(2,1)S(1)}, u32[]{:S(2)}, u32[]{:S(2)}) collective-permute-start(bf16[2,16,64,128]{3,2,1,0:T(8,128)(2,1)S(1)} %bitcast.47), channel_id=1, source_target_pairs={{0,1},{1,2},{2,3},{3,0},{4,5},{5,6},{6,7},{7,4},{8,9},{9,10},{10,1... | collective-permute-start | bytes 1572872 | tf_op jit(solution)/shard_map/ppermute | solution.py:364
  4.9 1.0 collective-permute-start.1
  6.0 1.2 copy.77
  7.2 1.1 collective-permute-start.2
  8.3 1.9 collective-permute-start.3
  10.2 1.2 copy.76
  12.0 2.5 %slice_reduce_fusion = (bf16[27,4096]{1,0:T(8,128)(2,1)S(1)}, bf16[27,4096]{1,0:T(8,128)(2,1)}) fusion(bf16[2,27,4096]{2,0,1:T(2,128)(2,1)S(1)} %copy-done.11), kind=kLoop, calls=%fused_computation.11 | loop fusion | bytes 884736 | tf_op jit(solution)/shard_map/slice | solution.py:394
  14.5 2.2 %reshape_squeeze.13 = bf16[3,3,3,64,64]{4,3,2,1,0:T(8,128)(2,1)} reshape(bf16[27,4096]{1,0:T(8,128)(2,1)} %get-tuple-element.41) | data formatting | bytes 442368 | tf_op jit(solution)/shard_map/reshape;squeeze | solution.py:346
  16.7 3.6 %slice_bitcast_fusion = bf16[10,27,4096]{2,1,0:T(8,128)(2,1)} fusion(bf16[1,1,12,27,4096]{4,3,2,1,0:T(8,128)(2,1)} %param.13), kind=kLoop, calls=%fused_computation.1 | loop fusion | bytes 4423680 | tf_op jit(solution)/shard_map/squeeze | solution.py:426
  20.3 0.8 reverse_bitcast_fusion
  21.1 2.1 %copy.55 = bf16[3,3,64,3,64]{4,3,2,1,0:T(4,128)(2,1)} copy(bf16[3,3,64,3,64]{2,4,1,3,0:T(8,128)(2,1)} %reverse_bitcast_fusion) | data formatting | bytes 442368 | tf_op jit(solution)/shard_map/transpose | solution.py:352
  23.2 2.2 %reshape.38.w_at = bf16[3,192,192]{2,1,0:T(8,128)(2,1)} reshape(bf16[3,3,64,3,64]{4,3,2,1,0:T(4,128)(2,1)} %copy.55) | data formatting | bytes 442368 | tf_op jit(solution)/shard_map/reshape | solution.py:352
  25.3 2.2 %copy.53 = bf16[3,3,64,3,64]{4,3,2,1,0:T(4,128)(2,1)} copy(bf16[3,3,64,3,64]{4,2,1,3,0:T(8,128)(2,1)} %bitcast.56) | data formatting | bytes 442368 | tf_op jit(solution)/shard_map/transpose | solution.py:347
  27.6 2.2 %reshape.36.w_a = bf16[3,192,192]{2,1,0:T(8,128)(2,1)} reshape(bf16[3,3,64,3,64]{4,3,2,1,0:T(4,128)(2,1)} %copy.53) | data formatting | bytes 442368 | tf_op jit(solution)/shard_map/reshape | solution.py:347
  29.7 1.2 reshape_squeeze.14
  31.0 1.8 reverse_bitcast_fusion.1
  32.8 2.1 %copy.54 = bf16[3,3,64,3,64]{4,3,2,1,0:T(4,128)(2,1)} copy(bf16[3,3,64,3,64]{2,4,1,3,0:T(8,128)(2,1)} %reverse_bitcast_fusion.1) | data formatting | bytes 442368 | tf_op jit(solution)/shard_map/transpose | solution.py:352
  34.9 2.2 %reshape.37.w_bt = bf16[3,192,192]{2,1,0:T(8,128)(2,1)} reshape(bf16[3,3,64,3,64]{4,3,2,1,0:T(4,128)(2,1)} %copy.54) | data formatting | bytes 442368 | tf_op jit(solution)/shard_map/reshape | solution.py:352
  37.1 1.7 copy.59.first
  39.6 1.7 copy.61.master
  42.6 0.8 copy-done.3
  43.3 2.5 %collective-permute-start.5 = (bf16[2,16,64,128]{3,2,1,0:T(8,128)(2,1)S(1)}, bf16[2,16,64,128]{3,2,1,0:T(8,128)(2,1)}, u32[]{:S(2)}, u32[]{:S(2)}) collective-permute-start(bf16[2,16,64,128]{3,2,1,0:T(8,128)(2,1)S(1)} %bitcast.44), channel_id=1, source_target_pairs={{1,0},{2,1},{3,2},{0,3},{5,4},{6,5},{7,6},{4,7},{9,8},{10,9},{11,1... | collective-permute-start | bytes 1572872 | tf_op jit(solution)/shard_map/ppermute | solution.py:365
  45.8 0.8 copy-done.5
  46.6 0.8 copy-done.7
  47.4 5.6 %collective-permute-done.3.cot_high = bf16[2,16,64,128]{3,2,1,0:T(8,128)(2,1)} collective-permute-done((bf16[2,16,64,128]{3,2,1,0:T(8,128)(2,1)S(1)}, bf16[2,16,64,128]{3,2,1,0:T(8,128)(2,1)}, u32[]{:S(2)}, u32[]{:S(2)}) %collective-permute-start.3) | collective-permute-done | bytes 524320 | tf_op jit(solution)/shard_map/ppermute | solution.py:365
  53.0 1.0 copy-done
  54.0 1.0 copy-done.1
  54.9 1.0 copy-done.2
  55.9 1.0 copy-done.4
  57.0 1.0 copy-done.6
  58.0 1.0 copy-done.8
  59.0 19.5 %decoder.1 = (bf16[2,16,64,128]{3,2,1,0:T(8,128)(2,1)S(1)}, f32[3,192,192]{2,1,0:T(8,128)S(1)}, f32[3,192,192]{2,1,0:T(8,128)S(1)}) custom-call(bf16[2,16,64,128]{3,2,1,0:T(8,128)(2,1)S(1)} %copy-done.4, bf16[2,16,64,128]{3,2,1,0:T(8,128)(2,1)S(1)} %bitcast.49, bf16[2,16,64,128]{3,2,1,0:T(8,128)(2,1)S(1)} %copy-done.6, ...), custom_call_target="tpu_custom_call" | custom-call | flops 13589544960 | bytes 8388608 | tf_op jit(solution)/shard_map/decoder/pallas_call | solution.py:400
  78.6 1.4 reshape.39
  80.0 1.4 copy.57
  81.7 1.4 reshape.40
  83.0 1.4 copy.58
  84.8 1.1 fusion
  85.9 3.7 %pad_maximum_fusion.grads = bf16[12,27,4096]{2,1,0:T(8,128)(2,1)} fusion(bf16[10,27,4096]{2,1,0:T(8,128)(2,1)} %slice_bitcast_fusion, bf16[2,27,4096]{2,1,0:T(8,128)(2,1)S(1)} %fusion), kind=kLoop, calls=%fused_computation | loop fusion | flops 1327104 | bytes 5308416 | tf_op jit(solution)/shard_map/concatenate | solution.py:426
  89.6 80.7 %owners.1 = (bf16[12,27,4096]{2,1,0:T(8,128)(2,1)}, f32[2,27,1024]{2,1,0:T(8,128)}, f32[2,27,1024]{2,1,0:T(8,128)}, f32[2,27,1024]{2,1,0:T(8,128)}) custom-call(s32[16]{0:T(128)} %get-tuple-element.15.tensor_of, f32[16]{0:T(128)} %convert_element_type.12.used, s32[12]{0:T(128)} %assignment.1, bf16[12,27,4096]{2,1,0:T(8,128)(2,1)} %pad_maximum_fusion.grads, ...), custom_call_target="tpu_custom_call" | custom-call | flops 16777216 | bytes 16777216 | tf_op jit(solution)/shard_map/owners/pallas_call | solution.py:430
  170.4 1.1 fusion.2
  173.9 12.7 %encoder.1 = bf16[2,16,64,128]{3,2,1,0:T(8,128)(2,1)S(1)} custom-call(bf16[2,16,64,128]{3,2,1,0:T(8,128)(2,1)} %collective-permute-done.4.low, bf16[2,16,64,128]{3,2,1,0:T(8,128)(2,1)S(1)} %bitcast.45, bf16[2,16,64,128]{3,2,1,0:T(8,128)(2,1)} %collective-permute-done.5.high, bf16[3,192,192]{2,1,0:T(8,128)(2,1)S(1)} %reshape.41.w_c, ...), custom_call_target="tpu_custom_call" | custom-call | flops 5435817984 | bytes 4194304 | tf_op jit(solution)/shard_map/encoder/pallas_call | solution.py:459
  186.6 1.1 copy.65
  187.7 0.9 copy.66
  188.6 0.9 copy.67
  189.4 0.9 copy.68
  190.3 1.1 copy.64
  191.4 1.7 copy.80
  (43 shorter events, 5.7 us)
Async XLA Ops:
  0.6 11.3 %copy-start.11 = (bf16[2,27,4096]{2,0,1:T(2,128)(2,1)S(1)}, bf16[2,27,4096]{2,0,1:T(2,128)(2,1)}, u32[]{:S(2)}) copy-start(bf16[2,27,4096]{2,0,1:T(2,128)(2,1)} %param.12) | copy-start | bytes 1327108
  1.9 40.6 %collective-permute-start = (bf16[2,16,64,128]{3,2,1,0:T(8,128)(2,1)S(1)}, bf16[2,16,64,128]{3,2,1,0:T(8,128)(2,1)S(1)}, u32[]{:S(2)}, u32[]{:S(2)}) collective-permute-start(bf16[2,16,64,128]{3,2,1,0:T(8,128)(2,1)S(1)} %bitcast.47), channel_id=1, source_target_pairs={{0,1},{1,2},{2,3},{3,0},{4,5},{5,6},{6,7},{7,4},{8,9},{9,10},{10,1... | collective-permute-start | bytes 1572872 | tf_op jit(solution)/shard_map/ppermute | solution.py:364
  4.9 40.9 %collective-permute-start.1 = (bf16[2,16,64,128]{3,2,1,0:T(8,128)(2,1)S(1)}, bf16[2,16,64,128]{3,2,1,0:T(8,128)(2,1)S(1)}, u32[]{:S(2)}, u32[]{:S(2)}) collective-permute-start(bf16[2,16,64,128]{3,2,1,0:T(8,128)(2,1)S(1)} %bitcast.48), channel_id=1, source_target_pairs={{1,0},{2,1},{3,2},{0,3},{5,4},{6,5},{7,6},{4,7},{9,8},{10,9},{11,1... | collective-permute-start | bytes 1572872 | tf_op jit(solution)/shard_map/ppermute | solution.py:365
  7.2 39.4 %collective-permute-start.2 = (bf16[2,16,64,128]{3,2,1,0:T(8,128)(2,1)S(1)}, bf16[2,16,64,128]{3,2,1,0:T(8,128)(2,1)S(1)}, u32[]{:S(2)}, u32[]{:S(2)}) collective-permute-start(bf16[2,16,64,128]{3,2,1,0:T(8,128)(2,1)S(1)} %bitcast.50), channel_id=1, source_target_pairs={{0,1},{1,2},{2,3},{3,0},{4,5},{5,6},{6,7},{7,4},{8,9},{9,10},{10,1... | collective-permute-start | bytes 1572872 | tf_op jit(solution)/shard_map/ppermute | solution.py:364
  8.3 44.8 %collective-permute-start.3 = (bf16[2,16,64,128]{3,2,1,0:T(8,128)(2,1)S(1)}, bf16[2,16,64,128]{3,2,1,0:T(8,128)(2,1)}, u32[]{:S(2)}, u32[]{:S(2)}) collective-permute-start(bf16[2,16,64,128]{3,2,1,0:T(8,128)(2,1)S(1)} %bitcast.51), channel_id=1, source_target_pairs={{1,0},{2,1},{3,2},{0,3},{5,4},{6,5},{7,6},{4,7},{9,8},{10,9},{11,1... | collective-permute-start | bytes 1572872 | tf_op jit(solution)/shard_map/ppermute | solution.py:365
  11.4 162.4 %collective-permute-start.4 = (bf16[2,16,64,128]{3,2,1,0:T(8,128)(2,1)S(1)}, bf16[2,16,64,128]{3,2,1,0:T(8,128)(2,1)}, u32[]{:S(2)}, u32[]{:S(2)}) collective-permute-start(bf16[2,16,64,128]{3,2,1,0:T(8,128)(2,1)S(1)} %bitcast.43), channel_id=1, source_target_pairs={{0,1},{1,2},{2,3},{3,0},{4,5},{5,6},{6,7},{7,4},{8,9},{9,10},{10,1... | collective-permute-start | bytes 1572872 | tf_op jit(solution)/shard_map/ppermute | solution.py:364
  16.7 3.6 %copy-start.10 = (bf16[3,3,3,64,64]{4,3,2,1,0:T(8,128)(2,1)S(1)}, bf16[3,3,3,64,64]{4,3,2,1,0:T(8,128)(2,1)}, u32[]{:S(2)}) copy-start(bf16[3,3,3,64,64]{4,3,2,1,0:T(8,128)(2,1)} %reshape_squeeze.13) | copy-start | bytes 663556
  27.6 13.7 %copy-start.16 = (s32[12]{0:T(128)S(1)}, s32[12]{0:T(128)}, u32[]{:S(2)}) copy-start(s32[12]{0:T(128)} %assignment.1) | copy-start | bytes 148
  31.0 7.8 %copy-start.15 = (f32[2,27,1024]{2,0,1:T(2,128)S(1)}, f32[2,27,1024]{2,0,1:T(2,128)}, u32[]{:S(2)}) copy-start(f32[2,27,1024]{2,0,1:T(2,128)} %param.16) | copy-start | bytes 663556
  42.6 0.8 copy-start.3
  43.3 130.5 %collective-permute-start.5 = (bf16[2,16,64,128]{3,2,1,0:T(8,128)(2,1)S(1)}, bf16[2,16,64,128]{3,2,1,0:T(8,128)(2,1)}, u32[]{:S(2)}, u32[]{:S(2)}) collective-permute-start(bf16[2,16,64,128]{3,2,1,0:T(8,128)(2,1)S(1)} %bitcast.44), channel_id=1, source_target_pairs={{1,0},{2,1},{3,2},{0,3},{5,4},{6,5},{7,6},{4,7},{9,8},{10,9},{11,1... | collective-permute-start | bytes 1572872 | tf_op jit(solution)/shard_map/ppermute | solution.py:365
  45.8 0.8 copy-start.5
  46.6 0.8 copy-start.7
  53.0 1.0 copy-start
  54.0 1.0 copy-start.1
  54.9 1.0 copy-start.2
  55.9 1.0 copy-start.4
  57.0 1.0 copy-start.6
  58.0 1.0 copy-start.8
  173.8 13.9 %copy-start.14 = (f32[2,27,1024]{2,1,0:T(8,128)S(1)}, f32[2,27,1024]{2,1,0:T(8,128)}, u32[]{:S(2)}) copy-start(f32[2,27,1024]{2,1,0:T(8,128)} %get-tuple-element.37) | copy-start | bytes 663556
  173.8 14.7 %copy-start.13 = (f32[2,27,1024]{2,1,0:T(8,128)S(1)}, f32[2,27,1024]{2,1,0:T(8,128)}, u32[]{:S(2)}) copy-start(f32[2,27,1024]{2,1,0:T(8,128)} %get-tuple-element.38) | copy-start | bytes 663556
  173.9 15.6 %copy-start.12 = (f32[2,27,1024]{2,1,0:T(8,128)S(1)}, f32[2,27,1024]{2,1,0:T(8,128)}, u32[]{:S(2)}) copy-start(f32[2,27,1024]{2,1,0:T(8,128)} %get-tuple-element.39) | copy-start | bytes 663556
  186.6 4.9 %copy-start.9 = (bf16[12,27,4096]{2,1,0:T(8,128)(2,1)S(1)}, bf16[12,27,4096]{2,1,0:T(8,128)(2,1)}, u32[]{:S(2)}) copy-start(bf16[12,27,4096]{2,1,0:T(8,128)(2,1)} %get-tuple-element.52) | copy-start | bytes 7962628
